TPU v7x, 32 devices: a whole 2x2x4 slice. The times are simulated.
32 devices in a mesh: lat: 4 (over y, x), lon: 8 (over z, core).
Axes of the slice: x: 2, y: 2, z: 4, core: 2. Of those that a mesh axis runs over, the one named last changes fastest.
Arguments:
- tracer: float32 [6, 16, 32, 1024], P(None, None, 'lat', 'lon'), may hold values from -6 to 6
- east_vel: float32 [16, 32, 1024], P(None, 'lat', 'lon'), may hold values from -0.25 to 0.25
- north_vel: float32 [16, 32, 1024], P(None, 'lat', 'lon'), may hold values from -0.25 to 0.25
- wet_mask: int32 [16, 32, 1024], P(None, 'lat', 'lon'), may hold values from 0 to 1, as said below
- bottom_level: int32 [32, 1024], P('lat', 'lon'), may hold values from 0 to 16, as said below
- vertical_mix: float32 [16, 32, 1024], P(None, 'lat', 'lon'), may hold values from 0.05 to 5
Outputs:
- updated: float32 [6, 16, 32, 1024], P(None, None, 'lat', 'lon')
Inputs may be any that keep to these rules, and one draw needn't show every extreme that they name: bottom_level is the number of levels above a column's sea floor; 0 on land. wet_mask is 0 at every level at or below its column's bottom_level.
All inputs are finite; a program needn't handle non-finite values.
Results may differ from a plain program's by a relative error of at most 0.00002.
Values sent between devices are 32-bit elements; how exact they have to be, the bound alone decides.
A program may use at most 64 MiB of HBM per device.

v0:
```python
import jax
import jax.numpy as jnp
from jax import lax
from jax.sharding import PartitionSpec as P

lateral_mixing = 0.08


def extended(cells, sides, width):
    for axis, dim in sides:
        count = lax.axis_size(axis)
        head = lax.slice_in_dim(cells, 0, width, axis=dim)
        tail = lax.slice_in_dim(cells, cells.shape[dim] - width, cells.shape[dim], axis=dim)
        cells = jnp.concatenate(
            [
                lax.ppermute(tail, axis, [(i, (i + 1) % count) for i in range(count)]),
                cells,
                lax.ppermute(head, axis, [((i + 1) % count, i) for i in range(count)]),
            ],
            axis=dim,
        )
    return cells


def flux_sum(tracer_pad, east_pad, north_pad, mask_pad):
    east_speed = 0.5 * (east_pad[..., 1:-1, :-1] + east_pad[..., 1:-1, 1:])
    east_open = mask_pad[..., 1:-1, :-1] * mask_pad[..., 1:-1, 1:]
    west_side = tracer_pad[..., 1:-1, :-1]
    east_side = tracer_pad[..., 1:-1, 1:]
    east_flux = east_open * (
        jnp.maximum(east_speed, 0.0) * west_side
        + jnp.minimum(east_speed, 0.0) * east_side
        - lateral_mixing * (east_side - west_side)
    )
    north_speed = 0.5 * (north_pad[..., :-1, 1:-1] + north_pad[..., 1:, 1:-1])
    north_open = mask_pad[..., :-1, 1:-1] * mask_pad[..., 1:, 1:-1]
    south_side = tracer_pad[..., :-1, 1:-1]
    north_side = tracer_pad[..., 1:, 1:-1]
    north_flux = north_open * (
        jnp.maximum(north_speed, 0.0) * south_side
        + jnp.minimum(north_speed, 0.0) * north_side
        - lateral_mixing * (north_side - south_side)
    )
    return mask_pad[..., 1:-1, 1:-1] * (
        east_flux[..., :-1] - east_flux[..., 1:] + north_flux[..., :-1, :] - north_flux[..., 1:, :]
    )


def solve_columns(rhs_field, couple):
    level_count = couple.shape[0]
    ratios = []
    values = []
    upper_c = couple[0]
    denom = 1.0 + upper_c
    ratio_prev = -upper_c / denom
    value_prev = rhs_field[..., 0, :, :] / denom
    ratios.append(ratio_prev)
    values.append(value_prev)
    for level_index in range(1, level_count):
        lower_c = couple[level_index - 1]
        upper_c = couple[level_index]
        denom = 1.0 + lower_c + upper_c + lower_c * ratio_prev
        ratio_prev = -upper_c / denom
        value_prev = (rhs_field[..., level_index, :, :] + lower_c * value_prev) / denom
        ratios.append(ratio_prev)
        values.append(value_prev)
    result_rows = [values[level_count - 1]]
    for level_index in range(level_count - 2, -1, -1):
        result_rows.append(values[level_index] - ratios[level_index] * result_rows[-1])
    return jnp.stack(result_rows[::-1], axis=-3)


def fold_fix(inner_field, padded, halo_depth, sign_factors):
    row_count = inner_field.shape[2]
    ghosts = padded[:, :, row_count : row_count + halo_depth, ::-1][:, :, ::-1, :]
    ghost_shape = ghosts.shape
    flat_rows = ghosts.reshape(-1)
    total_count = flat_rows.shape[0]
    group_size = lax.axis_size("lon")
    piece_len = (total_count + group_size - 1) // group_size
    flat_rows = flat_rows.reshape(group_size, piece_len)
    spread = lax.all_to_all(flat_rows, "lon", split_axis=0, concat_axis=0, tiled=True)
    returned = lax.all_to_all(spread[::-1], "lon", split_axis=0, concat_axis=0, tiled=True)
    ghosts = returned.reshape(-1).reshape(ghost_shape)
    is_top = lax.axis_index("lat") == lax.axis_size("lat") - 1
    is_south = lax.axis_index("lat") == 0
    north_rows = jnp.where(is_top, sign_factors * ghosts, padded[:, :, row_count + halo_depth :, :])
    south_old = padded[:, :, :halo_depth, :]
    south_rows = jnp.where(is_south, jnp.zeros_like(south_old), south_old)
    return jnp.concatenate(
        [south_rows, padded[:, :, halo_depth : row_count + halo_depth, :], north_rows], axis=2
    )


def on_device(tracer, east_vel, north_vel, wet_mask, bottom_level, vertical_mix):
    tracer_count = tracer.shape[0]
    mask_float = wet_mask.astype(jnp.float32)
    stacked = jnp.concatenate([tracer, east_vel[None], north_vel[None], mask_float[None]], axis=0)
    tracer_signs = jnp.ones((tracer_count, 1, 1, 1), jnp.float32)
    sign_full = jnp.concatenate(
        [tracer_signs, -jnp.ones((2, 1, 1, 1), jnp.float32), jnp.ones((1, 1, 1, 1), jnp.float32)],
        axis=0,
    )
    level_ids = lax.broadcasted_iota(jnp.int32, vertical_mix.shape, 0)
    couple = jnp.where(level_ids + 1 < bottom_level[None, :, :], vertical_mix, jnp.float32(0.0))
    padded = extended(stacked, (("lat", 2), ("lon", 3)), 1)
    padded = fold_fix(stacked, padded, 1, sign_full)
    tracer_pad = padded[:tracer_count]
    east_pad = padded[tracer_count]
    north_pad = padded[tracer_count + 1]
    mask_pad = padded[tracer_count + 2]
    section_one = tracer + flux_sum(tracer_pad, east_pad, north_pad, mask_pad)
    again = extended(section_one, (("lat", 2), ("lon", 3)), 1)
    again = fold_fix(section_one, again, 1, tracer_signs)
    section_two = 0.5 * (tracer + section_one + flux_sum(again, east_pad, north_pad, mask_pad))
    return solve_columns(section_two, couple)


def solution(mesh):
    in_specs = (
        P(None, None, "lat", "lon"),
        P(None, "lat", "lon"),
        P(None, "lat", "lon"),
        P(None, "lat", "lon"),
        P("lat", "lon"),
        P(None, "lat", "lon"),
    )
    out_specs = P(None, None, "lat", "lon")
    return jax.shard_map(
        on_device, mesh=mesh, in_specs=in_specs, out_specs=out_specs, check_vma=False
    )
```

profile of v0, /device:TPU:0, one launch (start us, length us, event | category | flops | bytes accessed | tf_op | source)
XLA Modules:
  0.0 96.4 jit_solution(584511828153476161)
XLA Ops:
  0.0 0.9 fusion.8
  0.9 1.1 %copy.27 = f32[6,16,8,128]{3,1,0,2:T(8,128)S(1)} copy(f32[6,16,8,128]{3,2,1,0:T(8,128)} %param.6) | data formatting | bytes 786432 | tf_op args[0]
  2.0 0.9 copy_bitcast_fusion.1
  2.9 3.9 %collective-permute-start.1 = (f32[9,16,1,128]{3,1,0,2:T(8,128)S(1)}, f32[9,16,1,128]{3,1,0,2:T(8,128)S(1)}, u32[]{:S(2)}, u32[]{:S(2)}) collective-permute-start(f32[9,16,1,128]{3,1,0,2:T(8,128)S(1)} %get-tuple-element.74), channel_id=1, source_target_pairs={{8,0},{16,8},{24,16},{0,24},{9,1},{17,9},{25,17},{1,25},{10,2},{18... | collective-permute-start | bytes 221192 | tf_op jit(solution)/shard_map/ppermute | solution.py:18
  7.0 0.6 fusion.27
  7.6 0.6 fusion.28
  8.2 0.6 fusion.29
  9.4 0.6 fusion.31
  10.0 0.6 fusion.32
  10.6 0.6 fusion.33
  11.2 0.6 fusion.34
  11.8 0.6 fusion.35
  12.4 0.6 fusion.36
  14.0 2.8 %collective-permute-start.3 = (f32[9,16,10,1]{1,3,2,0:T(1,128)S(1)}, f32[9,16,10,1]{1,3,2,0:T(1,128)S(1)}, u32[]{:S(2)}, u32[]{:S(2)}) collective-permute-start(f32[9,16,10,1]{1,3,2,0:T(1,128)S(1)} %copy.19), channel_id=1, source_target_pairs={{1,0},{2,1},{3,2},{4,3},{5,4},{6,5},{7,6},{0,7},{9,8},{10,9},{11,1... | collective-permute-start | bytes 17288 | tf_op jit(solution)/shard_map/ppermute | solution.py:18
  17.4 0.6 fusion.37
  18.5 0.6 copy.21
  19.1 3.6 %collective-permute-done.2 = f32[9,16,10,1]{1,3,2,0:T(1,128)S(1)} collective-permute-done((f32[9,16,10,1]{1,3,2,0:T(1,128)S(1)}, f32[9,16,10,1]{1,3,2,0:T(1,128)S(1)}, u32[]{:S(2)}, u32[]{:S(2)}) %collective-permute-start.2) | collective-permute-done | bytes 5792 | tf_op jit(solution)/shard_map/ppermute | solution.py:16
  22.7 0.6 copy.20
  23.3 0.6 pad_maximum_fusion
  23.9 1.1 %copy-done = f32[9,16,10,130]{3,1,0,2:T(8,128)} copy-done((f32[9,16,10,130]{3,1,0,2:T(8,128)}, f32[9,16,10,130]{3,1,0,2:T(8,128)S(1)}, u32[]{:S(2)}) %copy-start) | copy-done | bytes 748824
  25.3 0.8 all_to_all.38
  26.2 3.4 %all-to-all-start = ((f32[8,1,2340]{2,1,0:T(1,128)}), f32[8,1,2340]{2,1,0:T(1,128)S(1)}, u32[]{:S(2)}, u32[]{:S(2)}) async-start(f32[8,1,2340]{2,1,0:T(1,128)} %all_to_all.38), calls=%async_computation | async-start | bytes 155648 | tf_op jit(solution)/shard_map/all_to_all | solution.py:82
  29.5 0.6 fusion.38
  30.1 5.4 %all-to-all-done = f32[8,1,2340]{2,1,0:T(1,128)S(1)} async-done(((f32[8,1,2340]{2,1,0:T(1,128)}), f32[8,1,2340]{2,1,0:T(1,128)S(1)}, u32[]{:S(2)}, u32[]{:S(2)}) %all-to-all-start) | async-done | bytes 74912 | tf_op jit(solution)/shard_map/all_to_all | solution.py:82
  35.8 0.7 copy.23
  36.6 3.5 %all-to-all-start.1 = ((f32[8,1,2340]{2,1,0:T(1,128)}), f32[8,1,2340]{2,1,0:T(1,128)S(1)}, u32[]{:S(2)}, u32[]{:S(2)}) async-start(f32[8,1,2340]{2,1,0:T(1,128)} %copy.23), calls=%async_computation.1 | async-start | bytes 155648 | tf_op jit(solution)/shard_map/all_to_all | solution.py:83
  40.1 0.6 fusion.39
  40.7 1.4 %slice.350 = f32[9,16,8,130]{3,1,0,2:T(8,128)S(1)} slice(f32[9,16,10,130]{3,1,0,2:T(8,128)} %copy-done), slice={[0:9], [0:16], [1:9], [0:130]} | slice | bytes 1198080 | tf_op jit(solution)/shard_map/slice | solution.py:91
  42.0 4.0 %all-to-all-done.1 = f32[8,1,2340]{2,1,0:T(1,128)S(1)} async-done(((f32[8,1,2340]{2,1,0:T(1,128)}), f32[8,1,2340]{2,1,0:T(1,128)S(1)}, u32[]{:S(2)}, u32[]{:S(2)}) %all-to-all-start.1) | async-done | bytes 74912 | tf_op jit(solution)/shard_map/all_to_all | solution.py:83
  46.4 1.1 %slice_select_fusion.1 = (f32[9,16,1,130]{3,1,0,2:T(8,128)S(1)}, f32[9,16,1,130]{3,1,0,2:T(8,128)S(1)}) fusion(f32[9,16,10,130]{3,1,0,2:T(8,128)} %copy-done, pred[]{:T(512)S(6)} %eq.8, f32[9,16,1,130]{3,1,0,2:T(8,128)S(1)} %reshape_reshape.8, f32[9]{0:T(128)S(1)} %copy-done.55, pred[]{:T(512)S(6)} %eq.9), kind=kLoop, calls=%fused_computation.47 | loop fusion | flops 56160 | bytes 374438 | tf_op jit(solution)/shard_map/jit(_where)/select_n | solution.py:89
  49.1 0.6 copy-done.1
  49.9 2.7 %collective-permute-start.5 = (f32[6,16,1,128]{3,1,0,2:T(8,128)S(1)}, f32[6,16,1,128]{3,1,0,2:T(8,128)S(1)}, u32[]{:S(2)}, u32[]{:S(2)}) collective-permute-start(f32[6,16,1,128]{3,1,0,2:T(8,128)S(1)} %get-tuple-element.78), channel_id=1, source_target_pairs={{8,0},{16,8},{24,16},{0,24},{9,1},{17,9},{25,17},{1,25},{10,2},{18... | collective-permute-start | bytes 147464 | tf_op jit(solution)/shard_map/ppermute | solution.py:18
  52.6 0.6 fusion.40
  53.2 1.1 %collective-permute-done.5 = f32[6,16,1,128]{3,1,0,2:T(8,128)S(1)} collective-permute-done((f32[6,16,1,128]{3,1,0,2:T(8,128)S(1)}, f32[6,16,1,128]{3,1,0,2:T(8,128)S(1)}, u32[]{:S(2)}, u32[]{:S(2)}) %collective-permute-start.5) | collective-permute-done | bytes 49184 | tf_op jit(solution)/shard_map/ppermute | solution.py:18
  54.4 3.2 %collective-permute-done.4 = f32[6,16,1,128]{3,1,0,2:T(8,128)S(1)} collective-permute-done((f32[6,16,1,128]{3,1,0,2:T(8,128)S(1)}, f32[6,16,1,128]{3,1,0,2:T(8,128)S(1)}, u32[]{:S(2)}, u32[]{:S(2)}) %collective-permute-start.4) | collective-permute-done | bytes 49184 | tf_op jit(solution)/shard_map/ppermute | solution.py:16
  58.4 0.7 fusion.25
  59.1 10.2 %collective-permute-done.7 = f32[6,16,10,1]{3,1,0,2:T(8,128)S(1)} collective-permute-done((f32[6,16,10,1]{3,1,0,2:T(8,128)S(1)}, f32[6,16,10,1]{3,1,0,2:T(8,128)S(1)}, u32[]{:S(2)}, u32[]{:S(2)}) %collective-permute-start.7) | collective-permute-done | bytes 3872 | tf_op jit(solution)/shard_map/ppermute | solution.py:18
  69.3 1.7 %collective-permute-done.6 = f32[6,16,10,1]{3,1,0,2:T(8,128)S(1)} collective-permute-done((f32[6,16,10,1]{3,1,0,2:T(8,128)S(1)}, f32[6,16,10,1]{3,1,0,2:T(8,128)S(1)}, u32[]{:S(2)}, u32[]{:S(2)}) %collective-permute-start.6) | collective-permute-done | bytes 3872 | tf_op jit(solution)/shard_map/ppermute | solution.py:16
  71.4 0.8 all_to_all.39
  72.1 3.3 %all-to-all-start.2 = ((f32[8,1,1560]{2,1,0:T(1,128)}), f32[8,1,1560]{2,1,0:T(1,128)S(1)}, u32[]{:S(2)}, u32[]{:S(2)}) async-start(f32[8,1,1560]{2,1,0:T(1,128)} %all_to_all.39), calls=%async_computation.2 | async-start | bytes 106496 | tf_op jit(solution)/shard_map/all_to_all | solution.py:82
  75.5 1.2 %subtract_multiply_fusion = f32[6,16,8,129]{3,1,0,2:T(8,128)} fusion(f32[6,16,10,1]{3,1,0,2:T(8,128)S(1)} %collective-permute-done.7, f32[6,16,1,128]{3,1,0,2:T(8,128)S(1)} %collective-permute-done.5, f32[6,16,8,128]{3,1,0,2:T(8,128)S(1)} %fusion.4, f32[6,16,1,128]{3,1,0,2:T(8,128)S(1)} %collective-permute-done.4, ...), kind=kLoop, calls=%fused_computation.20 | loop fusion | flops 1287936 | bytes 1093632 | tf_op jit(solution)/shard_map/mul | solution.py:30
  76.7 4.6 %all-to-all-done.2 = f32[8,1,1560]{2,1,0:T(1,128)S(1)} async-done(((f32[8,1,1560]{2,1,0:T(1,128)}), f32[8,1,1560]{2,1,0:T(1,128)S(1)}, u32[]{:S(2)}, u32[]{:S(2)}) %all-to-all-start.2) | async-done | bytes 49952 | tf_op jit(solution)/shard_map/all_to_all | solution.py:82
  81.5 0.7 copy.29
  82.2 3.3 %all-to-all-start.3 = ((f32[8,1,1560]{2,1,0:T(1,128)}), f32[8,1,1560]{2,1,0:T(1,128)S(1)}, u32[]{:S(2)}, u32[]{:S(2)}) async-start(f32[8,1,1560]{2,1,0:T(1,128)} %copy.29), calls=%async_computation.3 | async-start | bytes 106496 | tf_op jit(solution)/shard_map/all_to_all | solution.py:83
  86.1 5.2 %all-to-all-done.3 = f32[8,1,1560]{2,1,0:T(1,128)S(1)} async-done(((f32[8,1,1560]{2,1,0:T(1,128)}), f32[8,1,1560]{2,1,0:T(1,128)S(1)}, u32[]{:S(2)}, u32[]{:S(2)}) %all-to-all-start.3) | async-done | bytes 49952 | tf_op jit(solution)/shard_map/all_to_all | solution.py:83
  92.0 0.7 copy-done.2
  93.5 0.6 fusion.10
  95.4 1.0 %copy.30 = f32[6,16,8,128]{3,2,1,0:T(8,128)} copy(f32[6,16,8,128]{3,1,0,2:T(8,128)S(1)} %stack.2) | data formatting | bytes 786432 | tf_op jit(solution)/shard_map/stack | solution.py:70
  (158 shorter events, 9.7 us)
Async XLA Ops:
  0.0 6.9 %copy-start.19 = (f32[16,8,128]{2,1,0:T(8,128)S(1)}, f32[16,8,128]{2,1,0:T(8,128)}, u32[]{:S(2)}) copy-start(f32[16,8,128]{2,1,0:T(8,128)} %param.11) | copy-start | bytes 196612
  0.0 6.9 %copy-start.54 = (s32[8,128]{1,0:T(8,128)S(1)}, s32[8,128]{1,0:T(8,128)}, u32[]{:S(2)}) copy-start(s32[8,128]{1,0:T(8,128)} %param.10) | copy-start | bytes 12292
  2.9 10.1 %collective-permute-start.1 = (f32[9,16,1,128]{3,1,0,2:T(8,128)S(1)}, f32[9,16,1,128]{3,1,0,2:T(8,128)S(1)}, u32[]{:S(2)}, u32[]{:S(2)}) collective-permute-start(f32[9,16,1,128]{3,1,0,2:T(8,128)S(1)} %get-tuple-element.74), channel_id=1, source_target_pairs={{8,0},{16,8},{24,16},{0,24},{9,1},{17,9},{25,17},{1,25},{10,2},{18... | collective-permute-start | bytes 221192 | tf_op jit(solution)/shard_map/ppermute | solution.py:18
  6.8 6.2 %collective-permute-start = (f32[9,16,1,128]{3,1,0,2:T(8,128)S(1)}, f32[9,16,1,128]{3,1,0,2:T(8,128)S(1)}, u32[]{:S(2)}, u32[]{:S(2)}) collective-permute-start(f32[9,16,1,128]{3,1,0,2:T(8,128)S(1)} %get-tuple-element.73), channel_id=1, source_target_pairs={{0,8},{8,16},{16,24},{24,0},{1,9},{9,17},{17,25},{25,1},{2,10},{10... | collective-permute-start | bytes 221192 | tf_op jit(solution)/shard_map/ppermute | solution.py:16
  7.0 33.1 %copy-start.5 = (f32[16,8,128]{2,1,0:T(8,128)}, f32[16,8,128]{2,1,0:T(8,128)S(1)}, u32[]{:S(2)}) copy-start(f32[16,8,128]{2,1,0:T(8,128)S(1)} %compare_select_fusion) | copy-start | bytes 196612
  7.6 5.8 %copy-start.20 = (f32[1,8,128]{2,1,0:T(8,128)}, f32[1,8,128]{2,1,0:T(8,128)S(1)}, u32[]{:S(2)}) copy-start(f32[1,8,128]{2,1,0:T(8,128)S(1)} %get-tuple-element.22) | copy-start | bytes 12292
  13.0 10.2 %copy-start.13 = (f32[9,16,1,128]{3,1,0,2:T(8,128)}, f32[9,16,1,128]{3,1,0,2:T(8,128)S(1)}, u32[]{:S(2)}) copy-start(f32[9,16,1,128]{3,1,0,2:T(8,128)S(1)} %collective-permute-done.1) | copy-start | bytes 221188
  13.0 10.2 %copy-start.15 = (f32[9,16,1,128]{3,1,0,2:T(8,128)}, f32[9,16,1,128]{3,1,0,2:T(8,128)S(1)}, u32[]{:S(2)}) copy-start(f32[9,16,1,128]{3,1,0,2:T(8,128)S(1)} %collective-permute-done) | copy-start | bytes 221188
  14.0 4.5 %collective-permute-start.3 = (f32[9,16,10,1]{1,3,2,0:T(1,128)S(1)}, f32[9,16,10,1]{1,3,2,0:T(1,128)S(1)}, u32[]{:S(2)}, u32[]{:S(2)}) collective-permute-start(f32[9,16,10,1]{1,3,2,0:T(1,128)S(1)} %copy.19), channel_id=1, source_target_pairs={{1,0},{2,1},{3,2},{4,3},{5,4},{6,5},{7,6},{0,7},{9,8},{10,9},{11,1... | collective-permute-start | bytes 17288 | tf_op jit(solution)/shard_map/ppermute | solution.py:18
  17.3 5.3 %collective-permute-start.2 = (f32[9,16,10,1]{1,3,2,0:T(1,128)S(1)}, f32[9,16,10,1]{1,3,2,0:T(1,128)S(1)}, u32[]{:S(2)}, u32[]{:S(2)}) collective-permute-start(f32[9,16,10,1]{1,3,2,0:T(1,128)S(1)} %copy.18), channel_id=1, source_target_pairs={{0,1},{1,2},{2,3},{3,4},{4,5},{5,6},{6,7},{7,0},{8,9},{9,10},{10,1... | collective-permute-start | bytes 17288 | tf_op jit(solution)/shard_map/ppermute | solution.py:16
  23.9 1.1 %copy-start = (f32[9,16,10,130]{3,1,0,2:T(8,128)}, f32[9,16,10,130]{3,1,0,2:T(8,128)S(1)}, u32[]{:S(2)}) copy-start(f32[9,16,10,130]{3,1,0,2:T(8,128)S(1)} %pad_maximum_fusion) | copy-start | bytes 2246404
  26.2 9.4 %all-to-all-start = ((f32[8,1,2340]{2,1,0:T(1,128)}), f32[8,1,2340]{2,1,0:T(1,128)S(1)}, u32[]{:S(2)}, u32[]{:S(2)}) async-start(f32[8,1,2340]{2,1,0:T(1,128)} %all_to_all.38), calls=%async_computation | async-start | bytes 155648 | tf_op jit(solution)/shard_map/all_to_all | solution.py:82
  36.6 9.8 %copy-start.55 = (f32[9]{0:T(128)S(1)}, f32[9]{0:T(128)}, u32[]{:S(2)}) copy-start(f32[9]{0:T(128)} %constant.13.clone.1) | copy-start | bytes 112
  36.6 9.5 %all-to-all-start.1 = ((f32[8,1,2340]{2,1,0:T(1,128)}), f32[8,1,2340]{2,1,0:T(1,128)S(1)}, u32[]{:S(2)}, u32[]{:S(2)}) async-start(f32[8,1,2340]{2,1,0:T(1,128)} %copy.23), calls=%async_computation.1 | async-start | bytes 155648 | tf_op jit(solution)/shard_map/all_to_all | solution.py:83
  47.8 1.3 %copy-start.17 = (f32[16,8,128]{2,0,1:T(8,128)}, f32[16,8,128]{2,0,1:T(8,128)S(1)}, u32[]{:S(2)}) copy-start(f32[16,8,128]{2,0,1:T(8,128)S(1)} %slice.353) | copy-start | bytes 196612
  47.8 0.9 copy-start.16
  48.0 1.0 %copy-start.3 = (f32[16,8,129]{2,0,1:T(8,128)}, f32[16,8,129]{2,0,1:T(8,128)S(1)}, u32[]{:S(2)}) copy-start(f32[16,8,129]{2,0,1:T(8,128)S(1)} %get-tuple-element.80) | copy-start | bytes 198148
  48.7 1.0 %copy-start.1 = (f32[6,16,8,128]{3,2,1,0:T(8,128)S(1)}, f32[6,16,8,128]{3,2,1,0:T(8,128)}, u32[]{:S(2)}) copy-start(f32[6,16,8,128]{3,2,1,0:T(8,128)} %param.6) | copy-start | bytes 1179652
  49.7 2.9 %copy-start.6 = (f32[16,8,128]{2,1,0:T(8,128)S(1)}, f32[16,8,128]{2,1,0:T(8,128)}, u32[]{:S(2)}) copy-start(f32[16,8,128]{2,1,0:T(8,128)} %copy-done.5) | copy-start | bytes 196612
  49.9 4.4 %collective-permute-start.5 = (f32[6,16,1,128]{3,1,0,2:T(8,128)S(1)}, f32[6,16,1,128]{3,1,0,2:T(8,128)S(1)}, u32[]{:S(2)}, u32[]{:S(2)}) collective-permute-start(f32[6,16,1,128]{3,1,0,2:T(8,128)S(1)} %get-tuple-element.78), channel_id=1, source_target_pairs={{8,0},{16,8},{24,16},{0,24},{9,1},{17,9},{25,17},{1,25},{10,2},{18... | collective-permute-start | bytes 147464 | tf_op jit(solution)/shard_map/ppermute | solution.py:18
  52.6 5.0 %collective-permute-start.4 = (f32[6,16,1,128]{3,1,0,2:T(8,128)S(1)}, f32[6,16,1,128]{3,1,0,2:T(8,128)S(1)}, u32[]{:S(2)}, u32[]{:S(2)}) collective-permute-start(f32[6,16,1,128]{3,1,0,2:T(8,128)S(1)} %get-tuple-element.77), channel_id=1, source_target_pairs={{0,8},{8,16},{16,24},{24,0},{1,9},{9,17},{17,25},{25,1},{2,10},{10... | collective-permute-start | bytes 147464 | tf_op jit(solution)/shard_map/ppermute | solution.py:16
  57.8 17.7 %copy-start.4 = (f32[16,8,129]{2,0,1:T(8,128)S(1)}, f32[16,8,129]{2,0,1:T(8,128)}, u32[]{:S(2)}) copy-start(f32[16,8,129]{2,0,1:T(8,128)} %copy-done.3) | copy-start | bytes 198148
  57.9 11.4 %collective-permute-start.7 = (f32[6,16,10,1]{3,1,0,2:T(8,128)S(1)}, f32[6,16,10,1]{3,1,0,2:T(8,128)S(1)}, u32[]{:S(2)}, u32[]{:S(2)}) collective-permute-start(f32[6,16,10,1]{3,1,0,2:T(8,128)S(1)} %get-tuple-element.76), channel_id=1, source_target_pairs={{1,0},{2,1},{3,2},{4,3},{5,4},{6,5},{7,6},{0,7},{9,8},{10,9},{11,1... | collective-permute-start | bytes 11528 | tf_op jit(solution)/shard_map/ppermute | solution.py:18
  57.9 13.0 %collective-permute-start.6 = (f32[6,16,10,1]{3,1,0,2:T(8,128)S(1)}, f32[6,16,10,1]{3,1,0,2:T(8,128)S(1)}, u32[]{:S(2)}, u32[]{:S(2)}) collective-permute-start(f32[6,16,10,1]{3,1,0,2:T(8,128)S(1)} %get-tuple-element.75), channel_id=1, source_target_pairs={{0,1},{1,2},{2,3},{3,4},{4,5},{5,6},{6,7},{7,0},{8,9},{9,10},{10,1... | collective-permute-start | bytes 11528 | tf_op jit(solution)/shard_map/ppermute | solution.py:16
  72.1 9.2 %all-to-all-start.2 = ((f32[8,1,1560]{2,1,0:T(1,128)}), f32[8,1,1560]{2,1,0:T(1,128)S(1)}, u32[]{:S(2)}, u32[]{:S(2)}) async-start(f32[8,1,1560]{2,1,0:T(1,128)} %all_to_all.39), calls=%async_computation.2 | async-start | bytes 106496 | tf_op jit(solution)/shard_map/all_to_all | solution.py:82
  82.2 9.1 %all-to-all-start.3 = ((f32[8,1,1560]{2,1,0:T(1,128)}), f32[8,1,1560]{2,1,0:T(1,128)S(1)}, u32[]{:S(2)}, u32[]{:S(2)}) async-start(f32[8,1,1560]{2,1,0:T(1,128)} %copy.29), calls=%async_computation.3 | async-start | bytes 106496 | tf_op jit(solution)/shard_map/all_to_all | solution.py:83
  86.0 5.7 %copy-start.8 = (f32[16,9,128]{2,0,1:T(8,128)S(1)}, f32[16,9,128]{2,0,1:T(8,128)}, u32[]{:S(2)}) copy-start(f32[16,9,128]{2,0,1:T(8,128)} %copy-done.7) | copy-start | bytes 221188
  86.0 5.7 %copy-start.10 = (f32[16,9,128]{2,0,1:T(8,128)S(1)}, f32[16,9,128]{2,0,1:T(8,128)}, u32[]{:S(2)}) copy-start(f32[16,9,128]{2,0,1:T(8,128)} %copy-done.9) | copy-start | bytes 221188
  86.0 5.7 %copy-start.12 = (f32[16,9,128]{2,0,1:T(8,128)S(1)}, f32[16,9,128]{2,0,1:T(8,128)}, u32[]{:S(2)}) copy-start(f32[16,9,128]{2,0,1:T(8,128)} %copy-done.11) | copy-start | bytes 221188
  91.6 1.1 %copy-start.2 = (f32[6,16,8,129]{3,1,0,2:T(8,128)S(1)}, f32[6,16,8,129]{3,1,0,2:T(8,128)}, u32[]{:S(2)}) copy-start(f32[6,16,8,129]{3,1,0,2:T(8,128)} %subtract_multiply_fusion) | copy-start | bytes 1188868
  91.6 1.1 %copy-start.18 = (f32[16,8,128]{2,0,1:T(8,128)S(1)}, f32[16,8,128]{2,0,1:T(8,128)}, u32[]{:S(2)}) copy-start(f32[16,8,128]{2,0,1:T(8,128)} %copy-done.17) | copy-start | bytes 196612
  92.9 1.3 %copy-start.22 = (f32[8,128]{1,0:T(8,128)S(1)}, f32[8,128]{1,0:T(8,128)}, u32[]{:S(2)}) copy-start(f32[8,128]{1,0:T(8,128)} %get-tuple-element.23) | copy-start | bytes 12292
  92.9 1.3 %copy-start.23 = (f32[8,128]{1,0:T(8,128)S(1)}, f32[8,128]{1,0:T(8,128)}, u32[]{:S(2)}) copy-start(f32[8,128]{1,0:T(8,128)} %get-tuple-element.25) | copy-start | bytes 12292
  92.9 1.3 %copy-start.24 = (f32[8,128]{1,0:T(8,128)S(1)}, f32[8,128]{1,0:T(8,128)}, u32[]{:S(2)}) copy-start(f32[8,128]{1,0:T(8,128)} %get-tuple-element.27) | copy-start | bytes 12292
  92.9 1.3 %copy-start.25 = (f32[8,128]{1,0:T(8,128)S(1)}, f32[8,128]{1,0:T(8,128)}, u32[]{:S(2)}) copy-start(f32[8,128]{1,0:T(8,128)} %get-tuple-element.29) | copy-start | bytes 12292
  92.9 1.3 %copy-start.26 = (f32[8,128]{1,0:T(8,128)S(1)}, f32[8,128]{1,0:T(8,128)}, u32[]{:S(2)}) copy-start(f32[8,128]{1,0:T(8,128)} %get-tuple-element.31) | copy-start | bytes 12292
  92.9 1.3 %copy-start.27 = (f32[8,128]{1,0:T(8,128)S(1)}, f32[8,128]{1,0:T(8,128)}, u32[]{:S(2)}) copy-start(f32[8,128]{1,0:T(8,128)} %get-tuple-element.33) | copy-start | bytes 12292
  92.9 1.3 %copy-start.28 = (f32[8,128]{1,0:T(8,128)S(1)}, f32[8,128]{1,0:T(8,128)}, u32[]{:S(2)}) copy-start(f32[8,128]{1,0:T(8,128)} %get-tuple-element.83) | copy-start | bytes 12292
  92.9 1.3 %copy-start.29 = (f32[8,128]{1,0:T(8,128)S(1)}, f32[8,128]{1,0:T(8,128)}, u32[]{:S(2)}) copy-start(f32[8,128]{1,0:T(8,128)} %get-tuple-element.35) | copy-start | bytes 12292
  92.9 1.3 %copy-start.30 = (f32[8,128]{1,0:T(8,128)S(1)}, f32[8,128]{1,0:T(8,128)}, u32[]{:S(2)}) copy-start(f32[8,128]{1,0:T(8,128)} %get-tuple-element.37) | copy-start | bytes 12292
  92.9 1.3 %copy-start.31 = (f32[8,128]{1,0:T(8,128)S(1)}, f32[8,128]{1,0:T(8,128)}, u32[]{:S(2)}) copy-start(f32[8,128]{1,0:T(8,128)} %get-tuple-element.39) | copy-start | bytes 12292
  93.0 1.3 %copy-start.32 = (f32[8,128]{1,0:T(8,128)S(1)}, f32[8,128]{1,0:T(8,128)}, u32[]{:S(2)}) copy-start(f32[8,128]{1,0:T(8,128)} %get-tuple-element.41) | copy-start | bytes 12292
  93.0 1.3 %copy-start.33 = (f32[8,128]{1,0:T(8,128)S(1)}, f32[8,128]{1,0:T(8,128)}, u32[]{:S(2)}) copy-start(f32[8,128]{1,0:T(8,128)} %get-tuple-element.43) | copy-start | bytes 12292
  93.0 1.3 %copy-start.34 = (f32[8,128]{1,0:T(8,128)S(1)}, f32[8,128]{1,0:T(8,128)}, u32[]{:S(2)}) copy-start(f32[8,128]{1,0:T(8,128)} %get-tuple-element.45) | copy-start | bytes 12292
  93.0 1.3 %copy-start.35 = (f32[8,128]{1,0:T(8,128)S(1)}, f32[8,128]{1,0:T(8,128)}, u32[]{:S(2)}) copy-start(f32[8,128]{1,0:T(8,128)} %get-tuple-element.47) | copy-start | bytes 12292
  93.0 1.3 %copy-start.36 = (f32[8,128]{1,0:T(8,128)S(1)}, f32[8,128]{1,0:T(8,128)}, u32[]{:S(2)}) copy-start(f32[8,128]{1,0:T(8,128)} %get-tuple-element.84) | copy-start | bytes 12292
  93.0 1.3 %copy-start.37 = (f32[8,128]{1,0:T(8,128)S(1)}, f32[8,128]{1,0:T(8,128)}, u32[]{:S(2)}) copy-start(f32[8,128]{1,0:T(8,128)} %get-tuple-element.99) | copy-start | bytes 12292
  93.0 1.3 %copy-start.53 = (f32[8,128]{1,0:T(8,128)S(1)}, f32[8,128]{1,0:T(8,128)}, u32[]{:S(2)}) copy-start(f32[8,128]{1,0:T(8,128)} %get-tuple-element.21) | copy-start | bytes 12292
  (20 other events, 13.9 us)
where the time goes:
time: 97.2 us; the launch traced here: 96.4 us
  waiting for transfers between devices  39.5 us (41%)
  starting transfers between devices  23.6 us (24%)
  other arithmetic  17.1 us (18%)
  local copies, waits for them, and re-layouts  15.3 us (16%)
    ppermute x4, waiting for transfers between devices, extended(): lax.ppermute(head, axis, [((i + 1) % count, i) for i in range(count)])  11.8 us
    all_to_all x2, waiting for transfers between devices, fold_fix(): lax.all_to_all(flat_rows, 'lon', split_axis=0, concat_axis=0, tiled=True)  9.98 us
    ppermute x4, starting transfers between devices, extended(): lax.ppermute(head, axis, [((i + 1) % count, i) for i in range(count)])  9.49 us
    all_to_all x2, waiting for transfers between devices, fold_fix(): lax.all_to_all(spread[::-1], 'lon', split_axis=0, concat_axis=0, tiled=True)  9.25 us
    ppermute x4, waiting for transfers between devices, extended(): lax.ppermute(tail, axis, [(i, (i + 1) % count) for i in range(count)])  8.49 us
    mul x14, other arithmetic, solve_columns(): ratios[level_index] * result_rows[-1]  8.48 us
    all_to_all x2, starting transfers between devices, fold_fix(): lax.all_to_all(spread[::-1], 'lon', split_axis=0, concat_axis=0, tiled=True)  6.83 us
    all_to_all x2, starting transfers between devices, fold_fix(): lax.all_to_all(flat_rows, 'lon', split_axis=0, concat_axis=0, tiled=True)  6.7 us
  transfers between devices with their start and end apart: 12, of which 10 were waited for; matrix products, arithmetic and copies ran while one was open for 14% of the time, Pallas kernels for 0%

commit v1 on v0

v1 whole, which is shorter than its diff:
```python
import functools

import jax
import jax.numpy as jnp
from jax import lax
from jax.experimental import pallas as pl
from jax.experimental.pallas import tpu as pltpu
from jax.sharding import PartitionSpec as P

lateral_mixing = 0.08
MESH = pl.DeviceIdType.MESH
HIGH = lax.Precision.HIGHEST
ROWS, COLS = 8, 128
UNROLL = 2


def over_levels(count, body, carry, backward=False):
    def some(step, carry):
        for part in range(UNROLL):
            level = step * UNROLL + part
            if backward:
                level = count - 1 - level
            carry = body(level, carry)
        return carry

    return lax.fori_loop(0, count // UNROLL, some, carry)


def kernel(
    nt, k, n_lat, n_lon,
    t_hbm, u_hbm, v_hbm, m_hbm, b_hbm, mix_hbm, out,
    t, u, v, mi, b, mix, m, s1, rhs, y, coef, edge, solve,
    ns_send, ns_recv, ew_send, ew_recv, ns_send2, ns_recv2, ew_send2, ew_recv2,
    load_sem, send_sem, recv_sem,
):
    lat, lon = lax.axis_index("lat"), lax.axis_index("lon")
    is_top = lat == n_lat - 1
    has_south = lat > 0
    east = lax.rem(lon + 1, n_lon)
    west = lax.rem(lon + n_lon - 1, n_lon)
    north_id = (jnp.where(is_top, lat, lat + 1), jnp.where(is_top, n_lon - 1 - lon, lon))
    south_id = (jnp.where(has_south, lat - 1, lat), lon)
    top_flag = jnp.where(is_top, 1, 0)
    cells = k * ROWS

    loads = [
        pltpu.make_async_copy(src, dst, load_sem.at[i])
        for i, (src, dst) in enumerate(
            ((t_hbm, t), (v_hbm, v), (m_hbm, mi), (u_hbm, u), (b_hbm, b), (mix_hbm, mix))
        )
    ]
    for load in loads:
        load.start()

    barrier = pltpu.get_barrier_semaphore()
    for target in ((lat, east), (lat, west), north_id):
        pl.semaphore_signal(barrier, inc=1, device_id=target, device_id_type=MESH)

    @pl.when(has_south)
    def _():
        pl.semaphore_signal(barrier, inc=1, device_id=south_id, device_id_type=MESH)

    @pl.when(jnp.logical_not(has_south))
    def _():
        ns_recv[0] = jnp.zeros_like(ns_recv[0])
        ns_recv2[0] = jnp.zeros_like(ns_recv2[0])

    lane = lax.broadcasted_iota(jnp.int32, (ROWS, COLS), 1)
    row = lax.broadcasted_iota(jnp.int32, (ROWS, COLS), 0)
    pick_row = lax.broadcasted_iota(jnp.int32, (16, COLS), 0)
    pick_lane = lax.broadcasted_iota(jnp.int32, (16, COLS), 1)

    def picker(f):
        chosen = ((pick_row == f) & (pick_lane == 0)) | ((pick_row == 8 + f) & (pick_lane == COLS - 1))
        return jnp.where(chosen, 1.0, 0.0).astype(jnp.float32)

    def pack_rows(fields, send, flip_at):
        for side, at in ((0, 0), (1, ROWS - 1)):
            for f, (ref, base) in enumerate(fields):
                send[side, pl.ds(f * k, k), :] = ref[pl.ds(base + at, k, stride=ROWS), :]

        @pl.when(is_top)
        def _():
            a = lax.broadcasted_iota(jnp.int32, (COLS, COLS), 0)
            c = lax.broadcasted_iota(jnp.int32, (COLS, COLS), 1)
            mirror = jnp.where(a + c == COLS - 1, 1.0, 0.0).astype(jnp.float32)
            turned = jnp.dot(send[1], mirror, precision=HIGH, preferred_element_type=jnp.float32)
            if flip_at is not None:
                at_row = lax.broadcasted_iota(jnp.int32, turned.shape, 0)
                flips = (at_row >= flip_at) & (at_row < flip_at + k)
                turned = jnp.where(flips, -turned, turned)
            send[1] = turned

    def pack_columns(fields, send):
        total = jnp.zeros((16, COLS), jnp.float32)
        for f, (ref, base) in enumerate(fields):
            total += lax.dot_general(
                picker(f), ref[pl.ds(base, cells), :], (((1,), (1,)), ((), ())),
                precision=HIGH, preferred_element_type=jnp.float32,
            )
        send[...] = total

    def unpack_columns(count, recv):
        turned = recv[...].T
        for f in range(count):
            y[pl.ds(f * cells, cells), :] = jnp.dot(
                turned, picker(f), precision=HIGH, preferred_element_type=jnp.float32
            )

    def remote(src, dst, phase, way, land, target):
        return pltpu.make_async_remote_copy(
            src_ref=src, dst_ref=dst, send_sem=send_sem.at[phase, way],
            recv_sem=recv_sem.at[phase, land], device_id=target, device_id_type=MESH,
        )

    def row_copies(phase, send, recv):
        north = remote(send.at[1], recv.at[top_flag], phase, 1, top_flag, north_id)
        south = remote(send.at[0], recv.at[1], phase, 0, 1, south_id)
        return north, south

    def column_copies(phase, send, recv):
        to_west = remote(send.at[pl.ds(0, 8)], recv.at[pl.ds(8, 8)], phase, 2, 2, (lat, west))
        to_east = remote(send.at[pl.ds(8, 8)], recv.at[pl.ds(0, 8)], phase, 3, 3, (lat, east))
        return to_west, to_east

    def start_rows(pair):
        pair[0].start()

        @pl.when(has_south)
        def _():
            pair[1].start()

    def rows_arrive(phase, send, recv):
        remote(send.at[1], recv.at[1], phase, 1, 1, north_id).wait_recv()

        @pl.when(has_south)
        def _():
            remote(send.at[0], recv.at[0], phase, 0, 0, south_id).wait_recv()

    def tile(ref, level, f=0):
        return ref[pl.ds(pl.multiple_of(f * cells + level * ROWS, ROWS), ROWS), :]

    def put(ref, level, value, f=0):
        ref[pl.ds(pl.multiple_of(f * cells + level * ROWS, ROWS), ROWS), :] = value

    for load in loads[:3]:
        load.wait()
    m[...] = mi[...].astype(jnp.float32)
    row_fields = [(t, f * cells) for f in range(nt)] + [(v, 0), (m, 0)]
    pack_rows(row_fields, ns_send, nt * k)
    pl.semaphore_wait(barrier, jnp.where(has_south, 4, 3))
    rows_one = row_copies(0, ns_send, ns_recv)
    start_rows(rows_one)
    loads[3].wait()
    pack_columns([(t, f * cells) for f in range(nt)] + [(u, 0), (m, 0)], ew_send)
    columns_one = column_copies(0, ew_send, ew_recv)
    for copy in columns_one:
        copy.start()
    for load in loads[4:]:
        load.wait()

    bottom = b[...]

    def inner_one(level, carry):
        lower, ratio = carry
        uu, vv, mm = tile(u, level), tile(v, level), tile(m, level)
        speed = 0.5 * (pltpu.roll(uu, 1, 1) + uu)
        is_open = jnp.where(lane == 0, 0.0, mm * pltpu.roll(mm, 1, 1))
        ahead = is_open * (jnp.maximum(speed, 0.0) + lateral_mixing)
        back = is_open * (lateral_mixing - jnp.minimum(speed, 0.0))
        c_west = ahead
        c_east = pltpu.roll(back, COLS - 1, 1)
        c_mid = -(back + pltpu.roll(ahead, COLS - 1, 1))
        speed = 0.5 * (pltpu.roll(vv, 1, 0) + vv)
        is_open = jnp.where(row == 0, 0.0, mm * pltpu.roll(mm, 1, 0))
        ahead = is_open * (jnp.maximum(speed, 0.0) + lateral_mixing)
        back = is_open * (lateral_mixing - jnp.minimum(speed, 0.0))
        c_south = ahead
        c_north = pltpu.roll(back, ROWS - 1, 0)
        c_mid = c_mid - (back + pltpu.roll(ahead, ROWS - 1, 0))
        for i, c in enumerate((c_west, c_east, c_south, c_north, c_mid)):
            put(coef, level, c, i)
        for f in range(nt):
            tt = tile(t, level, f)
            put(s1, level, tt + stencil(tt, c_west, c_east, c_south, c_north, c_mid), f)
        upper = jnp.where(level + 1 < bottom, tile(mix, level), 0.0)
        inverse = 1.0 / (1.0 + lower + upper + lower * ratio)
        ratio = -upper * inverse
        put(solve, level, inverse, 0)
        put(solve, level, ratio, 1)
        put(solve, level, lower * inverse, 2)
        return upper, ratio

    def stencil(tt, c_west, c_east, c_south, c_north, c_mid):
        return (
            (c_west * pltpu.roll(tt, 1, 1) + c_east * pltpu.roll(tt, COLS - 1, 1))
            + (c_south * pltpu.roll(tt, 1, 0) + c_north * pltpu.roll(tt, ROWS - 1, 0))
        ) + c_mid * tt

    zero = jnp.zeros((ROWS, COLS), jnp.float32)
    over_levels(k, inner_one, (zero, zero))

    for copy in columns_one:
        copy.wait_recv()
    unpack_columns(nt + 2, ew_recv)
    rows_arrive(0, ns_send, ns_recv)

    def outer_one(level, carry):
        def line(side, f):
            return ns_recv[side, pl.ds(f * k + level, 1), :]

        uu, vv, mm = tile(u, level), tile(v, level), tile(m, level)
        speed = 0.5 * (tile(y, level, nt) + uu)
        is_open = mm * tile(y, level, nt + 1)
        ahead = is_open * (jnp.maximum(speed, 0.0) + lateral_mixing)
        back = is_open * (lateral_mixing - jnp.minimum(speed, 0.0))
        c_side = jnp.where(lane < COLS // 2, ahead, back)
        c_more = -jnp.where(lane < COLS // 2, back, ahead)
        speed = 0.5 * (line(0, nt) + vv)
        is_open = jnp.where(row == 0, mm * line(0, nt + 1), 0.0)
        c_south = is_open * (jnp.maximum(speed, 0.0) + lateral_mixing)
        c_more = c_more - is_open * (lateral_mixing - jnp.minimum(speed, 0.0))
        speed = 0.5 * (line(1, nt) + vv)
        is_open = jnp.where(row == ROWS - 1, mm * line(1, nt + 1), 0.0)
        c_north = is_open * (lateral_mixing - jnp.minimum(speed, 0.0))
        c_more = c_more - is_open * (jnp.maximum(speed, 0.0) + lateral_mixing)
        put(edge, level, c_side, 0)
        put(edge, level, c_south, 1)
        put(edge, level, c_north, 2)
        put(coef, level, tile(coef, level, 4) + c_more, 4)
        for f in range(nt):
            added = (c_side * tile(y, level, f) + c_more * tile(t, level, f)) + (
                c_south * line(0, f) + c_north * line(1, f)
            )
            put(s1, level, tile(s1, level, f) + added, f)
        return carry

    over_levels(k, outer_one, 0)

    s1_fields = [(s1, f * cells) for f in range(nt)]
    pack_rows(s1_fields, ns_send2, None)
    rows_two = row_copies(1, ns_send2, ns_recv2)
    start_rows(rows_two)
    pack_columns(s1_fields, ew_send2)
    columns_two = column_copies(1, ew_send2, ew_recv2)
    for copy in columns_two:
        copy.start()

    def inner_two(level, carry):
        c = [tile(coef, level, i) for i in range(5)]
        for f in range(nt):
            ss = tile(s1, level, f)
            put(rhs, level, 0.5 * ((tile(t, level, f) + ss) + stencil(ss, *c)), f)
        return carry

    over_levels(k, inner_two, 0)

    for copy in columns_two:
        copy.wait_recv()
    unpack_columns(nt, ew_recv2)
    rows_arrive(1, ns_send2, ns_recv2)

    def forward(level, carry):
        def line(side, f):
            return ns_recv2[side, pl.ds(f * k + level, 1), :]

        c_side, c_south, c_north = (0.5 * tile(edge, level, i) for i in range(3))
        inverse, carried = tile(solve, level, 0), tile(solve, level, 2)
        now = []
        for f in range(nt):
            added = c_side * tile(y, level, f) + (c_south * line(0, f) + c_north * line(1, f))
            value = (tile(rhs, level, f) + added) * inverse + carried * carry[f]
            put(rhs, level, value, f)
            now.append(value)
        return tuple(now)

    over_levels(k, forward, (zero,) * nt)

    def backward(level, carry):
        ratio = tile(solve, level, 1)
        now = []
        for f in range(nt):
            value = tile(rhs, level, f) - ratio * carry[f]
            put(out, level, value, f)
            now.append(value)
        return tuple(now)

    over_levels(k, backward, (zero,) * nt, backward=True)

    for pair in (rows_one, rows_two):
        pair[0].wait_send()
    for copy in columns_one + columns_two:
        copy.wait_send()

    @pl.when(has_south)
    def _():
        rows_one[1].wait_send()
        rows_two[1].wait_send()


def on_device(n_lat, n_lon, tracer, east_vel, north_vel, wet_mask, bottom_level, vertical_mix):
    nt, k, rows, cols = tracer.shape
    cells = k * rows
    f32 = jnp.float32

    def vmem(*shape, dtype=f32):
        return pltpu.VMEM(shape, dtype)

    result = pl.pallas_call(
        functools.partial(kernel, nt, k, n_lat, n_lon),
        out_shape=jax.ShapeDtypeStruct((nt * cells, cols), f32),
        in_specs=[pl.BlockSpec(memory_space=pl.ANY)] * 6,
        out_specs=pl.BlockSpec(memory_space=pltpu.VMEM),
        scratch_shapes=[
            vmem(nt * cells, cols),
            vmem(cells, cols),
            vmem(cells, cols),
            vmem(cells, cols, dtype=jnp.int32),
            vmem(rows, cols, dtype=jnp.int32),
            vmem(cells, cols),
            vmem(cells, cols),
            vmem(nt * cells, cols),
            vmem(nt * cells, cols),
            vmem((nt + 2) * cells, cols),
            vmem(5 * cells, cols),
            vmem(3 * cells, cols),
            vmem(3 * cells, cols),
            vmem(2, (nt + 2) * k, cols),
            vmem(2, (nt + 2) * k, cols),
            vmem(16, cols),
            vmem(16, cols),
            vmem(2, nt * k, cols),
            vmem(2, nt * k, cols),
            vmem(16, cols),
            vmem(16, cols),
            pltpu.SemaphoreType.DMA((6,)),
            pltpu.SemaphoreType.DMA((2, 4)),
            pltpu.SemaphoreType.DMA((2, 4)),
        ],
        compiler_params=pltpu.CompilerParams(
            collective_id=0, has_side_effects=True, vmem_limit_bytes=32 * 1024 * 1024
        ),
    )(
        tracer.reshape(nt * cells, cols),
        east_vel.reshape(cells, cols),
        north_vel.reshape(cells, cols),
        wet_mask.reshape(cells, cols),
        bottom_level,
        vertical_mix.reshape(cells, cols),
    )
    return result.reshape(tracer.shape)


def solution(mesh):
    in_specs = (
        P(None, None, "lat", "lon"),
        P(None, "lat", "lon"),
        P(None, "lat", "lon"),
        P(None, "lat", "lon"),
        P("lat", "lon"),
        P(None, "lat", "lon"),
    )
    out_specs = P(None, None, "lat", "lon")
    return jax.shard_map(
        functools.partial(on_device, mesh.shape["lat"], mesh.shape["lon"]),
        mesh=mesh, in_specs=in_specs, out_specs=out_specs, check_vma=False,
    )
```

time: 97.2 us -> 22.3 us (0.23)
  waiting for transfers between devices: 39.5 us -> 0 us
  starting transfers between devices: 23.6 us -> 0 us
  other arithmetic: 17.1 us -> 0 us
  Pallas kernels: 0 us -> 16.1 us
  local copies, waits for them, and re-layouts: 15.3 us -> 5.79 us
    ppermute x8 -> x0, waiting for transfers between devices: 20.3 us -> none  [the longest x4 11.8 us: extended(): lax.ppermute(head, axis, [((i + 1) % count, i) for i in range(count)])]
    all_to_all x4 -> x0, waiting for transfers between devices: 19.2 us -> none  [the longest x2 9.98 us: fold_fix(): lax.all_to_all(flat_rows, 'lon', split_axis=0, concat_axis=0, tiled=True)]
    pallas_call x0 -> x1, Pallas kernels: none -> 16.1 us  [on_device(): pl.pallas_call(functools.partial(kernel, nt, k, n_lat, n_lon), out_shape=...]
    all_to_all x4 -> x0, starting transfers between devices: 13.5 us -> none  [the longest x2 6.83 us: fold_fix(): lax.all_to_all(spread[::-1], 'lon', split_axis=0, concat_axis=0, tiled=True)]
    mul x21 -> x0, other arithmetic: 11.1 us -> none  [the longest x14 8.48 us: solve_columns(): ratios[level_index] * result_rows[-1]]
    ppermute x8 -> x0, starting transfers between devices: 10 us -> none  [the longest x4 9.49 us: extended(): lax.ppermute(head, axis, [((i + 1) % count, i) for i in range(count)])]
    slice x9 -> x0, local copies, waits for them, and re-layouts: 3.13 us -> none  [the longest x2 1.41 us: fold_fix(): padded[:, :, halo_depth:row_count + halo_depth, :]]
    all_to_all x4 -> x0, local copies, waits for them, and re-layouts: 2.98 us -> none  [the longest x2 1.59 us: fold_fix(): lax.all_to_all(flat_rows, 'lon', split_axis=0, concat_axis=0, tiled=True)]
  transfers between devices with their start and end apart: 12 -> 0, of which waited for: 10 -> 0; matrix products, arithmetic and copies ran while one was open for 14% -> 0% of each run, Pallas kernels for 0% -> 0%
where the time goes in v1:
time: 22.3 us; the launch traced here: 21.9 us
  Pallas kernels  16.1 us (72%)
  local copies, waits for them, and re-layouts  5.79 us (26%)
    pallas_call x1, Pallas kernels, on_device(): pl.pallas_call(functools.partial(kernel, nt, k, n_lat, n_lon), out_shape=...  16.1 us
    unnamed x13, local copies, waits for them, and re-layouts  5.79 us

profile of v1, /device:TPU:0, one launch (start us, length us, event | category | flops | bytes accessed | tf_op | source)
XLA Modules:
  0.0 21.9 jit_solution(14783123523360659893)
XLA Ops:
  0.0 0.0 copy-start.5
  0.0 0.7 %copy-done.5 = s32[8,128]{1,0:T(8,128)S(1)} copy-done((s32[8,128]{1,0:T(8,128)S(1)}, s32[8,128]{1,0:T(8,128)}, u32[]{:S(2)}) %copy-start.5) | copy-done | bytes 4120
  0.7 0.0 copy-start
  0.7 1.0 %copy-done = f32[6,16,8,128]{3,2,1,0:T(8,128)S(1)} copy-done((f32[6,16,8,128]{3,2,1,0:T(8,128)S(1)}, f32[6,16,8,128]{3,2,1,0:T(8,128)}, u32[]{:S(2)}) %copy-start) | copy-done | bytes 393240
  1.7 0.0 copy-start.1
  1.7 0.8 %copy-done.1 = f32[16,8,128]{2,1,0:T(8,128)S(1)} copy-done((f32[16,8,128]{2,1,0:T(8,128)S(1)}, f32[16,8,128]{2,1,0:T(8,128)}, u32[]{:S(2)}) %copy-start.1) | copy-done | bytes 65560
  2.5 0.0 copy-start.2
  2.5 0.8 %copy-done.2 = f32[16,8,128]{2,1,0:T(8,128)S(1)} copy-done((f32[16,8,128]{2,1,0:T(8,128)S(1)}, f32[16,8,128]{2,1,0:T(8,128)}, u32[]{:S(2)}) %copy-start.2) | copy-done | bytes 65560
  3.4 0.0 copy-start.3
  3.4 0.8 %copy-done.3 = s32[16,8,128]{2,1,0:T(8,128)S(1)} copy-done((s32[16,8,128]{2,1,0:T(8,128)S(1)}, s32[16,8,128]{2,1,0:T(8,128)}, u32[]{:S(2)}) %copy-start.3) | copy-done | bytes 65560
  4.2 0.0 copy-start.4
  4.2 0.8 %copy-done.4 = f32[16,8,128]{2,1,0:T(8,128)S(1)} copy-done((f32[16,8,128]{2,1,0:T(8,128)S(1)}, f32[16,8,128]{2,1,0:T(8,128)}, u32[]{:S(2)}) %copy-start.4) | copy-done | bytes 65560
  5.0 16.1 %shard_map.64 = f32[768,128]{1,0:T(8,128)S(1)} custom-call(f32[768,128]{1,0:T(8,128)S(1)} %bitcast.7, f32[128,128]{1,0:T(8,128)S(1)} %bitcast.8, f32[128,128]{1,0:T(8,128)S(1)} %bitcast.9, s32[128,128]{1,0:T(8,128)S(1)} %bitcast.10, s32[8,128]{1,0:T(8,128)S(1)} %copy-done.5, f32[128,128]{1,0:T(8,128)S(1)} %bitcast.11), custom_call_target="tpu_custom_call" | custom-call | tf_op jit(solution)/shard_map/pallas_call | solution.py:309
  21.2 0.7 %copy.8 = f32[6,16,8,128]{3,2,1,0:T(8,128)} copy(f32[6,16,8,128]{3,2,1,0:T(8,128)S(1)} %bitcast.6) | data formatting | bytes 786432
Async XLA Ops:
  0.0 0.7 %copy-start.5 = (s32[8,128]{1,0:T(8,128)S(1)}, s32[8,128]{1,0:T(8,128)}, u32[]{:S(2)}) copy-start(s32[8,128]{1,0:T(8,128)} %b_hbm.1) | copy-start | bytes 12292
  0.7 1.0 %copy-start = (f32[6,16,8,128]{3,2,1,0:T(8,128)S(1)}, f32[6,16,8,128]{3,2,1,0:T(8,128)}, u32[]{:S(2)}) copy-start(f32[6,16,8,128]{3,2,1,0:T(8,128)} %param.6) | copy-start | bytes 1179652
  1.7 0.8 %copy-start.1 = (f32[16,8,128]{2,1,0:T(8,128)S(1)}, f32[16,8,128]{2,1,0:T(8,128)}, u32[]{:S(2)}) copy-start(f32[16,8,128]{2,1,0:T(8,128)} %param.7) | copy-start | bytes 196612
  2.5 0.8 %copy-start.2 = (f32[16,8,128]{2,1,0:T(8,128)S(1)}, f32[16,8,128]{2,1,0:T(8,128)}, u32[]{:S(2)}) copy-start(f32[16,8,128]{2,1,0:T(8,128)} %param.8) | copy-start | bytes 196612
  3.4 0.8 %copy-start.3 = (s32[16,8,128]{2,1,0:T(8,128)S(1)}, s32[16,8,128]{2,1,0:T(8,128)}, u32[]{:S(2)}) copy-start(s32[16,8,128]{2,1,0:T(8,128)} %param.9) | copy-start | bytes 196612
  4.2 0.8 %copy-start.4 = (f32[16,8,128]{2,1,0:T(8,128)S(1)}, f32[16,8,128]{2,1,0:T(8,128)}, u32[]{:S(2)}) copy-start(f32[16,8,128]{2,1,0:T(8,128)} %param.11) | copy-start | bytes 196612

commit v2 on v1

--- a/solution.py
+++ b/solution.py
@@ -12,14 +12,15 @@
 HIGH = lax.Precision.HIGHEST
 ROWS, COLS = 8, 128
 UNROLL = 2
-
-
-def over_levels(count, body, carry, backward=False):
+GROUPS = 4
+
+
+def over_levels(count, body, carry, last=None):
     def some(step, carry):
         for part in range(UNROLL):
             level = step * UNROLL + part
-            if backward:
-                level = count - 1 - level
+            if last is not None:
+                level = last - level
             carry = body(level, carry)
         return carry
 
@@ -31,7 +32,7 @@
     t_hbm, u_hbm, v_hbm, m_hbm, b_hbm, mix_hbm, out,
     t, u, v, mi, b, mix, m, s1, rhs, y, coef, edge, solve,
     ns_send, ns_recv, ew_send, ew_recv, ns_send2, ns_recv2, ew_send2, ew_recv2,
-    load_sem, send_sem, recv_sem,
+    load_sem, send_sem, recv_sem, store_sem,
 ):
     lat, lon = lax.axis_index("lat"), lax.axis_index("lon")
     is_top = lat == n_lat - 1
@@ -67,17 +68,12 @@
 
     lane = lax.broadcasted_iota(jnp.int32, (ROWS, COLS), 1)
     row = lax.broadcasted_iota(jnp.int32, (ROWS, COLS), 0)
-    pick_row = lax.broadcasted_iota(jnp.int32, (16, COLS), 0)
-    pick_lane = lax.broadcasted_iota(jnp.int32, (16, COLS), 1)
-
-    def picker(f):
-        chosen = ((pick_row == f) & (pick_lane == 0)) | ((pick_row == 8 + f) & (pick_lane == COLS - 1))
-        return jnp.where(chosen, 1.0, 0.0).astype(jnp.float32)
+    ends = (lane == 0) | (lane == COLS - 1)
 
     def pack_rows(fields, send, flip_at):
-        for side, at in ((0, 0), (1, ROWS - 1)):
+        for which, at in ((0, 0), (1, ROWS - 1)):
             for f, (ref, base) in enumerate(fields):
-                send[side, pl.ds(f * k, k), :] = ref[pl.ds(base + at, k, stride=ROWS), :]
+                send[which, pl.ds(f * k, k), :] = ref[pl.ds(base + at, k, stride=ROWS), :]
 
         @pl.when(is_top)
         def _():
@@ -92,20 +88,23 @@
             send[1] = turned
 
     def pack_columns(fields, send):
-        total = jnp.zeros((16, COLS), jnp.float32)
+        wide = lax.broadcasted_iota(jnp.int32, (cells, COLS), 1)
+        packed = None
         for f, (ref, base) in enumerate(fields):
-            total += lax.dot_general(
-                picker(f), ref[pl.ds(base, cells), :], (((1,), (1,)), ((), ())),
-                precision=HIGH, preferred_element_type=jnp.float32,
-            )
-        send[...] = total
-
-    def unpack_columns(count, recv):
-        turned = recv[...].T
-        for f in range(count):
-            y[pl.ds(f * cells, cells), :] = jnp.dot(
-                turned, picker(f), precision=HIGH, preferred_element_type=jnp.float32
-            )
+            moved = pltpu.roll(ref[pl.ds(base, cells), :], 2 * f + 1, 1)
+            packed = moved if f == 0 else jnp.where(wide >= 2 * f, moved, packed)
+        send[...] = packed.T[:16]
+
+    def unpack_columns(recv):
+        at_row = lax.broadcasted_iota(jnp.int32, (16, COLS), 0)
+        merged = jnp.where(
+            lax.rem(at_row, 2) == 0, pltpu.roll(recv[1], 15, 0), pltpu.roll(recv[0], 1, 0)
+        )
+        full = jnp.concatenate([merged, jnp.zeros((COLS - 16, COLS), jnp.float32)], axis=0)
+        y[...] = full.T
+
+    def side(level, f):
+        return pltpu.roll(tile(y, level), COLS - 1 - 2 * f, 1)
 
     def remote(src, dst, phase, way, land, target):
         return pltpu.make_async_remote_copy(
@@ -119,8 +118,8 @@
         return north, south
 
     def column_copies(phase, send, recv):
-        to_west = remote(send.at[pl.ds(0, 8)], recv.at[pl.ds(8, 8)], phase, 2, 2, (lat, west))
-        to_east = remote(send.at[pl.ds(8, 8)], recv.at[pl.ds(0, 8)], phase, 3, 3, (lat, east))
+        to_west = remote(send, recv.at[1], phase, 2, 2, (lat, west))
+        to_east = remote(send, recv.at[0], phase, 3, 3, (lat, east))
         return to_west, to_east
 
     def start_rows(pair):
@@ -142,17 +141,26 @@
 
     def put(ref, level, value, f=0):
         ref[pl.ds(pl.multiple_of(f * cells + level * ROWS, ROWS), ROWS), :] = value
+
+    def at_level(level):
+        return pl.ds(pl.multiple_of(level * ROWS, ROWS), ROWS)
+
+    def tile3(ref, level, f):
+        return ref[f, at_level(level), :]
+
+    def put3(ref, level, value, f):
+        ref[f, at_level(level), :] = value
 
     for load in loads[:3]:
         load.wait()
     m[...] = mi[...].astype(jnp.float32)
     row_fields = [(t, f * cells) for f in range(nt)] + [(v, 0), (m, 0)]
     pack_rows(row_fields, ns_send, nt * k)
+    loads[3].wait()
+    pack_columns([(t, f * cells) for f in range(nt)] + [(u, 0), (m, 0)], ew_send)
     pl.semaphore_wait(barrier, jnp.where(has_south, 4, 3))
     rows_one = row_copies(0, ns_send, ns_recv)
     start_rows(rows_one)
-    loads[3].wait()
-    pack_columns([(t, f * cells) for f in range(nt)] + [(u, 0), (m, 0)], ew_send)
     columns_one = column_copies(0, ew_send, ew_recv)
     for copy in columns_one:
         copy.start()
@@ -202,16 +210,16 @@
 
     for copy in columns_one:
         copy.wait_recv()
-    unpack_columns(nt + 2, ew_recv)
+    unpack_columns(ew_recv)
     rows_arrive(0, ns_send, ns_recv)
 
     def outer_one(level, carry):
-        def line(side, f):
-            return ns_recv[side, pl.ds(f * k + level, 1), :]
+        def line(which, f):
+            return ns_recv[which, pl.ds(f * k + level, 1), :]
 
         uu, vv, mm = tile(u, level), tile(v, level), tile(m, level)
-        speed = 0.5 * (tile(y, level, nt) + uu)
-        is_open = mm * tile(y, level, nt + 1)
+        speed = 0.5 * (side(level, nt) + uu)
+        is_open = jnp.where(ends, mm * side(level, nt + 1), 0.0)
         ahead = is_open * (jnp.maximum(speed, 0.0) + lateral_mixing)
         back = is_open * (lateral_mixing - jnp.minimum(speed, 0.0))
         c_side = jnp.where(lane < COLS // 2, ahead, back)
@@ -229,7 +237,7 @@
         put(edge, level, c_north, 2)
         put(coef, level, tile(coef, level, 4) + c_more, 4)
         for f in range(nt):
-            added = (c_side * tile(y, level, f) + c_more * tile(t, level, f)) + (
+            added = (c_side * side(level, f) + c_more * tile(t, level, f)) + (
                 c_south * line(0, f) + c_north * line(1, f)
             )
             put(s1, level, tile(s1, level, f) + added, f)
@@ -250,27 +258,27 @@
         c = [tile(coef, level, i) for i in range(5)]
         for f in range(nt):
             ss = tile(s1, level, f)
-            put(rhs, level, 0.5 * ((tile(t, level, f) + ss) + stencil(ss, *c)), f)
+            put3(rhs, level, (tile(t, level, f) + ss) + stencil(ss, *c), f)
         return carry
 
     over_levels(k, inner_two, 0)
 
     for copy in columns_two:
         copy.wait_recv()
-    unpack_columns(nt, ew_recv2)
+    unpack_columns(ew_recv2)
     rows_arrive(1, ns_send2, ns_recv2)
 
     def forward(level, carry):
-        def line(side, f):
-            return ns_recv2[side, pl.ds(f * k + level, 1), :]
-
-        c_side, c_south, c_north = (0.5 * tile(edge, level, i) for i in range(3))
+        def line(which, f):
+            return ns_recv2[which, pl.ds(f * k + level, 1), :]
+
+        c_side, c_south, c_north = (tile(edge, level, i) for i in range(3))
         inverse, carried = tile(solve, level, 0), tile(solve, level, 2)
         now = []
         for f in range(nt):
-            added = c_side * tile(y, level, f) + (c_south * line(0, f) + c_north * line(1, f))
-            value = (tile(rhs, level, f) + added) * inverse + carried * carry[f]
-            put(rhs, level, value, f)
+            added = c_side * side(level, f) + (c_south * line(0, f) + c_north * line(1, f))
+            value = (tile3(rhs, level, f) + added) * inverse + carried * carry[f]
+            put3(rhs, level, value, f)
             now.append(value)
         return tuple(now)
 
@@ -280,13 +288,22 @@
         ratio = tile(solve, level, 1)
         now = []
         for f in range(nt):
-            value = tile(rhs, level, f) - ratio * carry[f]
-            put(out, level, value, f)
+            value = tile3(rhs, level, f) - ratio * carry[f]
+            put3(rhs, level, value, f)
             now.append(value)
         return tuple(now)
 
-    over_levels(k, backward, (zero,) * nt, backward=True)
-
+    carry = (zero,) * nt
+    share = k // GROUPS
+    stores = []
+    for group in reversed(range(GROUPS)):
+        carry = over_levels(share, backward, carry, last=(group + 1) * share - 1)
+        span = (slice(None), pl.ds(group * share * ROWS, share * ROWS), slice(None))
+        stores.append(pltpu.make_async_copy(rhs.at[span], out.at[span], store_sem.at[group]))
+        stores[-1].start()
+
+    for store in stores:
+        store.wait()
     for pair in (rows_one, rows_two):
         pair[0].wait_send()
     for copy in columns_one + columns_two:
@@ -308,9 +325,9 @@
 
     result = pl.pallas_call(
         functools.partial(kernel, nt, k, n_lat, n_lon),
-        out_shape=jax.ShapeDtypeStruct((nt * cells, cols), f32),
-        in_specs=[pl.BlockSpec(memory_space=pl.ANY)] * 6,
-        out_specs=pl.BlockSpec(memory_space=pltpu.VMEM),
+        out_shape=jax.ShapeDtypeStruct((nt, cells, cols), f32),
+        in_specs=[pl.BlockSpec(memory_space=pltpu.HBM)] * 6,
+        out_specs=pl.BlockSpec(memory_space=pltpu.HBM),
         scratch_shapes=[
             vmem(nt * cells, cols),
             vmem(cells, cols),
@@ -320,25 +337,26 @@
             vmem(cells, cols),
             vmem(cells, cols),
             vmem(nt * cells, cols),
-            vmem(nt * cells, cols),
-            vmem((nt + 2) * cells, cols),
+            vmem(nt, cells, cols),
+            vmem(cells, cols),
             vmem(5 * cells, cols),
             vmem(3 * cells, cols),
             vmem(3 * cells, cols),
             vmem(2, (nt + 2) * k, cols),
             vmem(2, (nt + 2) * k, cols),
             vmem(16, cols),
-            vmem(16, cols),
+            vmem(2, 16, cols),
             vmem(2, nt * k, cols),
             vmem(2, nt * k, cols),
             vmem(16, cols),
-            vmem(16, cols),
+            vmem(2, 16, cols),
             pltpu.SemaphoreType.DMA((6,)),
             pltpu.SemaphoreType.DMA((2, 4)),
             pltpu.SemaphoreType.DMA((2, 4)),
+            pltpu.SemaphoreType.DMA((GROUPS,)),
         ],
         compiler_params=pltpu.CompilerParams(
-            collective_id=0, has_side_effects=True, vmem_limit_bytes=32 * 1024 * 1024
+            collective_id=0, has_side_effects=True, vmem_limit_bytes=62 * 1024 * 1024
         ),
     )(
         tracer.reshape(nt * cells, cols),
@@ -348,7 +366,7 @@
         bottom_level,
         vertical_mix.reshape(cells, cols),
     )
-    return result.reshape(tracer.shape)
+    return 0.5 * result.reshape(tracer.shape)
 
 
 def solution(mesh):

time: 22.3 us -> 17.4 us (0.78)
  local copies, waits for them, and re-layouts: 5.79 us -> 0 us
  other arithmetic: 0 us -> 1.77 us
  Pallas kernels: 16.1 us -> 15.4 us
    unnamed x13 -> x0, local copies, waits for them, and re-layouts: 5.79 us -> none
    mul x0 -> x1, other arithmetic: none -> 1.77 us  [on_device(): return 0.5 * result.reshape(tracer.shape)]
    pallas_call x1, Pallas kernels: 16.1 us -> 15.4 us  [on_device(): pl.pallas_call(functools.partial(kernel, nt, k, n_lat, n_lon), out_shape=...]
where the time goes in v2:
time: 17.4 us; the launch traced here: 17.2 us
  Pallas kernels  15.4 us (89%)
  other arithmetic  1.77 us (10%)
    pallas_call x1, Pallas kernels, on_device(): pl.pallas_call(functools.partial(kernel, nt, k, n_lat, n_lon), out_shape=...  15.4 us
    mul x1, other arithmetic, on_device(): return 0.5 * result.reshape(tracer.shape)  1.77 us

profile of v2, /device:TPU:0, one launch (start us, length us, event | category | flops | bytes accessed | tf_op | source)
XLA Modules:
  0.0 17.2 jit_solution(12555811087050963021)
XLA Ops:
  0.0 15.4 %shard_map.64 = f32[6,128,128]{2,1,0:T(8,128)} custom-call(f32[768,128]{1,0:T(8,128)} %bitcast.7, f32[128,128]{1,0:T(8,128)} %bitcast.8, f32[128,128]{1,0:T(8,128)} %bitcast.9, s32[128,128]{1,0:T(8,128)} %bitcast.10, s32[8,128]{1,0:T(8,128)} %b_hbm.1, f32[128,128]{1,0:T(8,128)} %bitcast.11), custom_call_target="tpu_custom_call" | custom-call | tf_op jit(solution)/shard_map/pallas_call | solution.py:326
  15.5 1.8 %multiply_bitcast_fusion = f32[6,16,8,128]{3,2,1,0:T(8,128)} fusion(f32[6,128,128]{2,1,0:T(8,128)} %shard_map.64), kind=kLoop, calls=%fused_computation | loop fusion | flops 98304 | bytes 786432 | tf_op jit(solution)/shard_map/mul | solution.py:369

commit v3 on v2

v3 whole, which is shorter than its diff:
```python
import functools

import jax
import jax.numpy as jnp
from jax import lax
from jax.experimental import pallas as pl
from jax.experimental.pallas import tpu as pltpu
from jax.sharding import PartitionSpec as P

lateral_mixing = 0.08
MESH = pl.DeviceIdType.MESH
HIGH = lax.Precision.HIGHEST
ROWS, COLS = 8, 128
GROUPS = 3


def over_levels(count, body, carry, unroll, backward=False):
    def some(step, carry):
        for part in range(unroll):
            level = step * unroll + part
            carry = body(count - 1 - level if backward else level, carry)
        return carry

    if unroll == count:
        return some(0, carry)
    return lax.fori_loop(0, count // unroll, some, carry)


def kernel(
    nt, k, n_lat, n_lon,
    t_hbm, u_hbm, v_hbm, m_hbm, b_hbm, mix_hbm, out,
    t, u, v, mi, b, mix, m, s1, rhs, y, y2, coef, edge, solve,
    ns_send, ns_recv, ew_send, ew_recv, ns_send2, ns_recv2, ew_send2, ew_recv2,
    load_sem, send_sem, recv_sem,
):
    lat, lon = lax.axis_index("lat"), lax.axis_index("lon")
    is_top = lat == n_lat - 1
    has_south = lat > 0
    east = lax.rem(lon + 1, n_lon)
    west = lax.rem(lon + n_lon - 1, n_lon)
    north_id = (jnp.where(is_top, lat, lat + 1), jnp.where(is_top, n_lon - 1 - lon, lon))
    south_id = (jnp.where(has_south, lat - 1, lat), lon)
    top_flag = jnp.where(is_top, 1, 0)
    cells = k * ROWS

    loads = [
        pltpu.make_async_copy(src, dst, load_sem.at[i])
        for i, (src, dst) in enumerate(
            ((t_hbm, t), (v_hbm, v), (m_hbm, mi), (u_hbm, u), (b_hbm, b), (mix_hbm, mix))
        )
    ]
    for load in loads:
        load.start()

    barrier = pltpu.get_barrier_semaphore()
    for target in ((lat, east), (lat, west), north_id):
        pl.semaphore_signal(barrier, inc=1, device_id=target, device_id_type=MESH)

    @pl.when(has_south)
    def _():
        pl.semaphore_signal(barrier, inc=1, device_id=south_id, device_id_type=MESH)

    @pl.when(jnp.logical_not(has_south))
    def _():
        ns_recv[0] = jnp.zeros_like(ns_recv[0])
        ns_recv2[0] = jnp.zeros_like(ns_recv2[0])

    lane = lax.broadcasted_iota(jnp.int32, (ROWS, COLS), 1)
    row = lax.broadcasted_iota(jnp.int32, (ROWS, COLS), 0)
    ends = (lane == 0) | (lane == COLS - 1)

    def pack_rows(fields, send, start, flip):
        for which, at in ((0, 0), (1, ROWS - 1)):
            for f, (ref, base) in enumerate(fields):
                send[which, pl.ds(start + f * k, k), :] = ref[pl.ds(base + at, k, stride=ROWS), :]

        @pl.when(is_top)
        def _():
            a = lax.broadcasted_iota(jnp.int32, (COLS, COLS), 0)
            c = lax.broadcasted_iota(jnp.int32, (COLS, COLS), 1)
            mirror = jnp.where(a + c == COLS - 1, 1.0, 0.0).astype(jnp.float32)
            span = pl.ds(start, len(fields) * k)
            send[1, span, :] = jnp.dot(
                send[1, span, :], mirror, precision=HIGH, preferred_element_type=jnp.float32
            )
            if flip:
                send[1, pl.ds(start, k), :] = -send[1, pl.ds(start, k), :]

    def pack_columns(fields, send):
        wide = lax.broadcasted_iota(jnp.int32, (cells, COLS), 1)
        packed = None
        for f, (ref, base) in enumerate(fields):
            moved = pltpu.roll(ref[pl.ds(base, cells), :], 2 * f + 1, 1)
            packed = moved if f == 0 else jnp.where(wide >= 2 * f, moved, packed)
        send[...] = packed.T[: send.shape[0]]

    def unpack_columns(recv, into):
        lines = recv.shape[1]
        at_row = lax.broadcasted_iota(jnp.int32, (lines, COLS), 0)
        merged = jnp.where(
            lax.rem(at_row, 2) == 0, pltpu.roll(recv[1], lines - 1, 0), pltpu.roll(recv[0], 1, 0)
        )
        full = jnp.concatenate([merged, jnp.zeros((COLS - lines, COLS), jnp.float32)], axis=0)
        into[...] = full.T

    def side(ref, level, f):
        return pltpu.roll(tile(ref, level), COLS - 1 - 2 * f, 1)

    def remote(src, dst, phase, group, way, land, target):
        return pltpu.make_async_remote_copy(
            src_ref=src, dst_ref=dst, send_sem=send_sem.at[phase, group, way],
            recv_sem=recv_sem.at[phase, group, land], device_id=target, device_id_type=MESH,
        )

    def row_copies(phase, group, send, recv, span):
        north = remote(send.at[1, span], recv.at[top_flag, span], phase, group, 1, top_flag, north_id)
        south = remote(send.at[0, span], recv.at[1, span], phase, group, 0, 1, south_id)
        return north, south

    def column_copies(phase, group, send, recv):
        to_west = remote(send, recv.at[1], phase, group, 2, 2, (lat, west))
        to_east = remote(send, recv.at[0], phase, group, 3, 3, (lat, east))
        return to_west, to_east

    def start_rows(pair):
        pair[0].start()

        @pl.when(has_south)
        def _():
            pair[1].start()

    def rows_arrive(phase, group, send, recv, span):
        remote(send.at[1, span], recv.at[1, span], phase, group, 1, 1, north_id).wait_recv()

        @pl.when(has_south)
        def _():
            remote(send.at[0, span], recv.at[0, span], phase, group, 0, 0, south_id).wait_recv()

    per = nt // GROUPS
    groups = range(GROUPS)
    spans_one = [pl.ds(0, (2 + per) * k)] + [pl.ds((2 + g * per) * k, per * k) for g in groups[1:]]
    spans_two = [pl.ds(g * per * k, per * k) for g in groups]

    def place(level, f=0):
        if isinstance(level, int):
            return pl.ds(f * cells + level * ROWS, ROWS)
        return pl.ds(pl.multiple_of(f * cells + level * ROWS, ROWS), ROWS)

    def tile(ref, level, f=0):
        return ref[place(level, f), :]

    def put(ref, level, value, f=0):
        ref[place(level, f), :] = value

    for load in loads[:3]:
        load.wait()
    m[...] = mi[...].astype(jnp.float32)
    rows_one = []
    for g in groups:
        fields = [(t, f * cells) for f in range(g * per, (g + 1) * per)]
        if g == 0:
            fields = [(v, 0), (m, 0)] + fields
        pack_rows(fields, ns_send, spans_one[g].start, g == 0)
        if g == 0:
            pl.semaphore_wait(barrier, jnp.where(has_south, 4, 3))
        rows_one.append(row_copies(0, g, ns_send, ns_recv, spans_one[g]))
        start_rows(rows_one[g])
        if g == 0:
            loads[3].wait()
            pack_columns([(t, f * cells) for f in range(nt)] + [(u, 0), (m, 0)], ew_send)
            columns_one = column_copies(0, 0, ew_send, ew_recv)
            for copy in columns_one:
                copy.start()
    for load in loads[4:]:
        load.wait()

    bottom = b[...]

    def inner_one(level, carry):
        lower, ratio = carry
        uu, vv, mm = tile(u, level), tile(v, level), tile(m, level)
        speed = 0.5 * (pltpu.roll(uu, 1, 1) + uu)
        is_open = jnp.where(lane == 0, 0.0, mm * pltpu.roll(mm, 1, 1))
        ahead = is_open * (jnp.maximum(speed, 0.0) + lateral_mixing)
        back = is_open * (lateral_mixing - jnp.minimum(speed, 0.0))
        c_west = ahead
        c_east = pltpu.roll(back, COLS - 1, 1)
        c_mid = -(back + pltpu.roll(ahead, COLS - 1, 1))
        speed = 0.5 * (pltpu.roll(vv, 1, 0) + vv)
        is_open = jnp.where(row == 0, 0.0, mm * pltpu.roll(mm, 1, 0))
        ahead = is_open * (jnp.maximum(speed, 0.0) + lateral_mixing)
        back = is_open * (lateral_mixing - jnp.minimum(speed, 0.0))
        c_south = ahead
        c_north = pltpu.roll(back, ROWS - 1, 0)
        c_mid = c_mid - (back + pltpu.roll(ahead, ROWS - 1, 0))
        for i, c in enumerate((c_west, c_east, c_south, c_north, c_mid)):
            put(coef, level, c, i)
        for f in range(nt):
            tt = tile(t, level, f)
            put(s1, level, tt + stencil(tt, c_west, c_east, c_south, c_north, c_mid), f)
        upper = jnp.where(level + 1 < bottom, tile(mix, level), 0.0)
        inverse = 1.0 / (1.0 + lower + upper + lower * ratio)
        ratio = -upper * inverse
        put(solve, level, inverse, 0)
        put(solve, level, ratio, 1)
        put(solve, level, lower * inverse, 2)
        return upper, ratio

    def stencil(tt, c_west, c_east, c_south, c_north, c_mid):
        return (
            (c_west * pltpu.roll(tt, 1, 1) + c_east * pltpu.roll(tt, COLS - 1, 1))
            + (c_south * pltpu.roll(tt, 1, 0) + c_north * pltpu.roll(tt, ROWS - 1, 0))
        ) + c_mid * tt

    zero = jnp.zeros((ROWS, COLS), jnp.float32)
    over_levels(k, inner_one, (zero, zero), 4)

    for copy in columns_one:
        copy.wait_recv()
    unpack_columns(ew_recv, y)

    def line(which, level, f):
        return ns_recv[which, pl.ds((2 + f) * k + level, 1), :]

    def outer_faces(level, carry):
        uu, vv, mm = tile(u, level), tile(v, level), tile(m, level)
        speed = 0.5 * (side(y, level, nt) + uu)
        is_open = jnp.where(ends, mm * side(y, level, nt + 1), 0.0)
        ahead = is_open * (jnp.maximum(speed, 0.0) + lateral_mixing)
        back = is_open * (lateral_mixing - jnp.minimum(speed, 0.0))
        c_side = jnp.where(lane < COLS // 2, ahead, back)
        c_more = -jnp.where(lane < COLS // 2, back, ahead)
        speed = 0.5 * (line(0, level, -2) + vv)
        is_open = jnp.where(row == 0, mm * line(0, level, -1), 0.0)
        c_south = is_open * (jnp.maximum(speed, 0.0) + lateral_mixing)
        c_more = c_more - is_open * (lateral_mixing - jnp.minimum(speed, 0.0))
        speed = 0.5 * (line(1, level, -2) + vv)
        is_open = jnp.where(row == ROWS - 1, mm * line(1, level, -1), 0.0)
        c_north = is_open * (lateral_mixing - jnp.minimum(speed, 0.0))
        c_more = c_more - is_open * (jnp.maximum(speed, 0.0) + lateral_mixing)
        for i, c in enumerate((c_side, c_south, c_north, c_more)):
            put(edge, level, c, i)
        put(coef, level, tile(coef, level, 4) + c_more, 4)
        return carry

    rows_two, columns_two = [], []
    for g in groups:
        mine = range(g * per, (g + 1) * per)

        def outer_one(level, carry):
            c_side, c_south, c_north, c_more = (tile(edge, level, i) for i in range(4))
            for f in mine:
                added = (c_side * side(y, level, f) + c_more * tile(t, level, f)) + (
                    c_south * line(0, level, f) + c_north * line(1, level, f)
                )
                put(s1, level, tile(s1, level, f) + added, f)
            return carry

        def inner_two(level, carry):
            c = [tile(coef, level, i) for i in range(5)]
            for f in mine:
                ss = tile(s1, level, f)
                put(rhs, level, 0.5 * ((tile(t, level, f) + ss) + stencil(ss, *c)), f)
            return carry

        rows_arrive(0, g, ns_send, ns_recv, spans_one[g])
        if g == 0:
            over_levels(k, outer_faces, 0, 8)
        over_levels(k, outer_one, 0, k)
        fields = [(s1, f * cells) for f in mine]
        pack_rows(fields, ns_send2, g * per * k, False)
        rows_two.append(row_copies(1, g, ns_send2, ns_recv2, spans_two[g]))
        start_rows(rows_two[g])
        pack_columns(fields, ew_send2.at[g])
        columns_two.append(column_copies(1, g, ew_send2.at[g], ew_recv2.at[g]))
        for copy in columns_two[g]:
            copy.start()
        over_levels(k, inner_two, 0, 8)

    for g in groups:
        mine = range(g * per, (g + 1) * per)
        sides = y2.at[g]

        def forward(level, carry):
            c_side, c_south, c_north = (0.5 * tile(edge, level, i) for i in range(3))
            inverse, carried = tile(solve, level, 0), tile(solve, level, 2)
            now = []
            for i, f in enumerate(mine):
                south = ns_recv2[0, pl.ds(f * k + level, 1), :]
                north = ns_recv2[1, pl.ds(f * k + level, 1), :]
                added = c_side * side(sides, level, i) + (c_south * south + c_north * north)
                value = (tile(rhs, level, f) + added) * inverse + carried * carry[i]
                put(rhs, level, value, f)
                now.append(value)
            return tuple(now)

        def backward(level, carry):
            ratio = tile(solve, level, 1)
            now = []
            for i, f in enumerate(mine):
                value = tile(rhs, level, f) - ratio * carry[i]
                put(out, level, value, f)
                now.append(value)
            return tuple(now)

        for copy in columns_two[g]:
            copy.wait_recv()
        unpack_columns(ew_recv2.at[g], sides)
        rows_arrive(1, g, ns_send2, ns_recv2, spans_two[g])
        over_levels(k, forward, (zero,) * per, k)
        over_levels(k, backward, (zero,) * per, k, backward=True)

    for copy in columns_one:
        copy.wait_send()
    for g in groups:
        rows_one[g][0].wait_send()
        rows_two[g][0].wait_send()
        for copy in columns_two[g]:
            copy.wait_send()

    @pl.when(has_south)
    def _():
        for pair in rows_one + rows_two:
            pair[1].wait_send()


def on_device(n_lat, n_lon, tracer, east_vel, north_vel, wet_mask, bottom_level, vertical_mix):
    nt, k, rows, cols = tracer.shape
    cells = k * rows
    f32 = jnp.float32

    def vmem(*shape, dtype=f32):
        return pltpu.VMEM(shape, dtype)

    result = pl.pallas_call(
        functools.partial(kernel, nt, k, n_lat, n_lon),
        out_shape=pltpu.VMEM((nt * cells, cols), f32),
        in_specs=[pl.BlockSpec(memory_space=pltpu.HBM)] * 6,
        out_specs=pl.BlockSpec(memory_space=pltpu.VMEM),
        scratch_shapes=[
            vmem(nt * cells, cols),
            vmem(cells, cols),
            vmem(cells, cols),
            vmem(cells, cols, dtype=jnp.int32),
            vmem(rows, cols, dtype=jnp.int32),
            vmem(cells, cols),
            vmem(cells, cols),
            vmem(nt * cells, cols),
            vmem(nt * cells, cols),
            vmem(cells, cols),
            vmem(GROUPS, cells, cols),
            vmem(5 * cells, cols),
            vmem(4 * cells, cols),
            vmem(3 * cells, cols),
            vmem(2, (nt + 2) * k, cols),
            vmem(2, (nt + 2) * k, cols),
            vmem(16, cols),
            vmem(2, 16, cols),
            vmem(2, nt * k, cols),
            vmem(2, nt * k, cols),
            vmem(GROUPS, 8, cols),
            vmem(GROUPS, 2, 8, cols),
            pltpu.SemaphoreType.DMA((6,)),
            pltpu.SemaphoreType.DMA((2, GROUPS, 4)),
            pltpu.SemaphoreType.DMA((2, GROUPS, 4)),
        ],
        compiler_params=pltpu.CompilerParams(
            collective_id=0, has_side_effects=True, vmem_limit_bytes=62 * 1024 * 1024
        ),
    )(
        tracer.reshape(nt * cells, cols),
        east_vel.reshape(cells, cols),
        north_vel.reshape(cells, cols),
        wet_mask.reshape(cells, cols),
        bottom_level,
        vertical_mix.reshape(cells, cols),
    )
    return result.reshape(tracer.shape)


def solution(mesh):
    in_specs = (
        P(None, None, "lat", "lon"),
        P(None, "lat", "lon"),
        P(None, "lat", "lon"),
        P(None, "lat", "lon"),
        P("lat", "lon"),
        P(None, "lat", "lon"),
    )
    out_specs = P(None, None, "lat", "lon")
    return jax.shard_map(
        functools.partial(on_device, mesh.shape["lat"], mesh.shape["lon"]),
        mesh=mesh, in_specs=in_specs, out_specs=out_specs, check_vma=False,
    )
```

time: 17.4 us -> 14.4 us (0.83)
  Pallas kernels: 15.4 us -> 13.5 us
  other arithmetic: 1.77 us -> 0 us
  local copies, waits for them, and re-layouts: 0 us -> 0.75 us
    pallas_call x1, Pallas kernels: 15.4 us -> 13.5 us  [on_device(): pl.pallas_call(functools.partial(kernel, nt, k, n_lat, n_lon), out_shape=...]
    mul x1 -> x0, other arithmetic: 1.77 us -> none  [on_device(): return 0.5 * result.reshape(tracer.shape)]
    unnamed x0 -> x1, local copies, waits for them, and re-layouts: none -> 0.75 us
where the time goes in v3:
time: 14.4 us; the launch traced here: 14.3 us
  Pallas kernels  13.5 us (94%)
  local copies, waits for them, and re-layouts  0.75 us (5%)
    pallas_call x1, Pallas kernels, on_device(): pl.pallas_call(functools.partial(kernel, nt, k, n_lat, n_lon), out_shape=...  13.5 us
    unnamed x1, local copies, waits for them, and re-layouts  0.75 us

profile of v3, /device:TPU:0, one launch (start us, length us, event | category | flops | bytes accessed | tf_op | source)
XLA Modules:
  0.0 14.3 jit_solution(10334757628569753330)
XLA Ops:
  0.0 13.5 %shard_map.64 = f32[768,128]{1,0:T(8,128)S(1)} custom-call(f32[768,128]{1,0:T(8,128)} %bitcast.7, f32[128,128]{1,0:T(8,128)} %bitcast.8, f32[128,128]{1,0:T(8,128)} %bitcast.9, s32[128,128]{1,0:T(8,128)} %bitcast.10, s32[8,128]{1,0:T(8,128)} %b_hbm.1, f32[128,128]{1,0:T(8,128)} %bitcast.11), custom_call_target="tpu_custom_call" | custom-call | tf_op jit(solution)/shard_map/pallas_call | solution.py:335
  13.5 0.7 %copy.8 = f32[6,16,8,128]{3,2,1,0:T(8,128)} copy(f32[6,16,8,128]{3,2,1,0:T(8,128)S(1)} %bitcast.6) | data formatting | bytes 786432

commit v4 on v3

--- a/solution.py
+++ b/solution.py
@@ -9,7 +9,6 @@
 
 lateral_mixing = 0.08
 MESH = pl.DeviceIdType.MESH
-HIGH = lax.Precision.HIGHEST
 ROWS, COLS = 8, 128
 GROUPS = 3
 
@@ -78,33 +77,41 @@
         def _():
             a = lax.broadcasted_iota(jnp.int32, (COLS, COLS), 0)
             c = lax.broadcasted_iota(jnp.int32, (COLS, COLS), 1)
-            mirror = jnp.where(a + c == COLS - 1, 1.0, 0.0).astype(jnp.float32)
+            mirror = jnp.where(a + c == COLS - 1, 1.0, 0.0).astype(jnp.bfloat16)
             span = pl.ds(start, len(fields) * k)
-            send[1, span, :] = jnp.dot(
-                send[1, span, :], mirror, precision=HIGH, preferred_element_type=jnp.float32
-            )
+            rest = send[1, span, :]
+            turned = None
+            for _ in range(3):
+                piece = rest.astype(jnp.bfloat16)
+                rest = rest - piece.astype(jnp.float32)
+                part = jnp.dot(piece, mirror, preferred_element_type=jnp.float32)
+                turned = part if turned is None else turned + part
+            send[1, span, :] = turned
             if flip:
                 send[1, pl.ds(start, k), :] = -send[1, pl.ds(start, k), :]
 
+    each = COLS // (2 * k)
+
     def pack_columns(fields, send):
-        wide = lax.broadcasted_iota(jnp.int32, (cells, COLS), 1)
-        packed = None
-        for f, (ref, base) in enumerate(fields):
-            moved = pltpu.roll(ref[pl.ds(base, cells), :], 2 * f + 1, 1)
-            packed = moved if f == 0 else jnp.where(wide >= 2 * f, moved, packed)
-        send[...] = packed.T[: send.shape[0]]
+        for block in range(send.shape[0]):
+            packed = None
+            for f, (ref, base) in enumerate(fields[block * each : (block + 1) * each]):
+                for level in range(k):
+                    at = 2 * (f * k + level)
+                    moved = pltpu.roll(ref[pl.ds(base + level * ROWS, ROWS), :], at + 1, 1)
+                    packed = moved if at == 0 else jnp.where(lane >= at, moved, packed)
+            send[block] = packed
 
     def unpack_columns(recv, into):
-        lines = recv.shape[1]
-        at_row = lax.broadcasted_iota(jnp.int32, (lines, COLS), 0)
-        merged = jnp.where(
-            lax.rem(at_row, 2) == 0, pltpu.roll(recv[1], lines - 1, 0), pltpu.roll(recv[0], 1, 0)
-        )
-        full = jnp.concatenate([merged, jnp.zeros((COLS - lines, COLS), jnp.float32)], axis=0)
-        into[...] = full.T
+        for block in range(recv.shape[1]):
+            into[block] = jnp.where(
+                lax.rem(lane, 2) == 0,
+                pltpu.roll(recv[1, block], COLS - 1, 1),
+                pltpu.roll(recv[0, block], 1, 1),
+            )
 
     def side(ref, level, f):
-        return pltpu.roll(tile(ref, level), COLS - 1 - 2 * f, 1)
+        return pltpu.roll(ref[f // each], COLS - 1 - 2 * (f % each * k + level), 1)
 
     def remote(src, dst, phase, group, way, land, target):
         return pltpu.make_async_remote_copy(
@@ -265,7 +272,7 @@
 
         rows_arrive(0, g, ns_send, ns_recv, spans_one[g])
         if g == 0:
-            over_levels(k, outer_faces, 0, 8)
+            over_levels(k, outer_faces, 0, k)
         over_levels(k, outer_one, 0, k)
         fields = [(s1, f * cells) for f in mine]
         pack_rows(fields, ns_send2, g * per * k, False)
@@ -328,6 +335,7 @@
     nt, k, rows, cols = tracer.shape
     cells = k * rows
     f32 = jnp.float32
+    blocks = (nt + 2) * k * 2 // cols
 
     def vmem(*shape, dtype=f32):
         return pltpu.VMEM(shape, dtype)
@@ -347,19 +355,19 @@
             vmem(cells, cols),
             vmem(nt * cells, cols),
             vmem(nt * cells, cols),
-            vmem(cells, cols),
-            vmem(GROUPS, cells, cols),
+            vmem(blocks, rows, cols),
+            vmem(GROUPS, 1, rows, cols),
             vmem(5 * cells, cols),
             vmem(4 * cells, cols),
             vmem(3 * cells, cols),
             vmem(2, (nt + 2) * k, cols),
             vmem(2, (nt + 2) * k, cols),
-            vmem(16, cols),
-            vmem(2, 16, cols),
+            vmem(blocks, rows, cols),
+            vmem(2, blocks, rows, cols),
             vmem(2, nt * k, cols),
             vmem(2, nt * k, cols),
-            vmem(GROUPS, 8, cols),
-            vmem(GROUPS, 2, 8, cols),
+            vmem(GROUPS, 1, rows, cols),
+            vmem(GROUPS, 2, 1, rows, cols),
             pltpu.SemaphoreType.DMA((6,)),
             pltpu.SemaphoreType.DMA((2, GROUPS, 4)),
             pltpu.SemaphoreType.DMA((2, GROUPS, 4)),

time: 14.4 us -> 14.2 us (0.986)
  Pallas kernels: 13.5 us -> 13.3 us
    pallas_call x1, Pallas kernels: 13.5 us -> 13.3 us  [on_device(): pl.pallas_call(functools.partial(kernel, nt, k, n_lat, n_lon), out_shape=...]
where the time goes in v4:
time: 14.2 us; the launch traced here: 14.1 us
  Pallas kernels  13.3 us (94%)
  local copies, waits for them, and re-layouts  0.75 us (5%)
    pallas_call x1, Pallas kernels, on_device(): pl.pallas_call(functools.partial(kernel, nt, k, n_lat, n_lon), out_shape=...  13.3 us
    unnamed x1, local copies, waits for them, and re-layouts  0.75 us

profile of v4, /device:TPU:0, one launch (start us, length us, event | category | flops | bytes accessed | tf_op | source)
XLA Modules:
  0.0 14.1 jit_solution(718116386892756535)
XLA Ops:
  0.0 13.3 %shard_map.64 = f32[768,128]{1,0:T(8,128)S(1)} custom-call(f32[768,128]{1,0:T(8,128)} %bitcast.7, f32[128,128]{1,0:T(8,128)} %bitcast.8, f32[128,128]{1,0:T(8,128)} %bitcast.9, s32[128,128]{1,0:T(8,128)} %bitcast.10, s32[8,128]{1,0:T(8,128)} %b_hbm.1, f32[128,128]{1,0:T(8,128)} %bitcast.11), custom_call_target="tpu_custom_call" | custom-call | tf_op jit(solution)/shard_map/pallas_call | solution.py:343
  13.3 0.7 %copy.8 = f32[6,16,8,128]{3,2,1,0:T(8,128)} copy(f32[6,16,8,128]{3,2,1,0:T(8,128)S(1)} %bitcast.6) | data formatting | bytes 786432

commit v5 on v4

--- a/solution.py
+++ b/solution.py
@@ -27,9 +27,9 @@
 
 def kernel(
     nt, k, n_lat, n_lon,
-    t_hbm, u_hbm, v_hbm, m_hbm, b_hbm, mix_hbm, out,
+    t_hbm, u_hbm, v_hbm, m_hbm, b_hbm, mix_hbm, t_rows, v_rows, m_rows, out,
     t, u, v, mi, b, mix, m, s1, rhs, y, y2, coef, edge, solve,
-    ns_send, ns_recv, ew_send, ew_recv, ns_send2, ns_recv2, ew_send2, ew_recv2,
+    ns_recv, mask_recv, wide_mask, ew_send, ew_recv, ns_send2, ns_recv2, ew_send2, ew_recv2,
     load_sem, send_sem, recv_sem,
 ):
     lat, lon = lax.axis_index("lat"), lax.axis_index("lon")
@@ -63,32 +63,35 @@
     def _():
         ns_recv[0] = jnp.zeros_like(ns_recv[0])
         ns_recv2[0] = jnp.zeros_like(ns_recv2[0])
+        mask_recv[0] = jnp.zeros_like(mask_recv[0])
 
     lane = lax.broadcasted_iota(jnp.int32, (ROWS, COLS), 1)
     row = lax.broadcasted_iota(jnp.int32, (ROWS, COLS), 0)
     ends = (lane == 0) | (lane == COLS - 1)
 
-    def pack_rows(fields, send, start, flip):
+    def pack_rows(fields, send, start):
         for which, at in ((0, 0), (1, ROWS - 1)):
             for f, (ref, base) in enumerate(fields):
                 send[which, pl.ds(start + f * k, k), :] = ref[pl.ds(base + at, k, stride=ROWS), :]
 
+    def mirrored(rest):
+        a = lax.broadcasted_iota(jnp.int32, (COLS, COLS), 0)
+        c = lax.broadcasted_iota(jnp.int32, (COLS, COLS), 1)
+        mirror = jnp.where(a + c == COLS - 1, 1.0, 0.0).astype(jnp.bfloat16)
+        turned = None
+        for _ in range(3):
+            piece = rest.astype(jnp.bfloat16)
+            rest = rest - piece.astype(jnp.float32)
+            part = jnp.dot(piece, mirror, preferred_element_type=jnp.float32)
+            turned = part if turned is None else turned + part
+        return turned
+
+    def fold_rows(recv, start, count, flip=False):
         @pl.when(is_top)
         def _():
-            a = lax.broadcasted_iota(jnp.int32, (COLS, COLS), 0)
-            c = lax.broadcasted_iota(jnp.int32, (COLS, COLS), 1)
-            mirror = jnp.where(a + c == COLS - 1, 1.0, 0.0).astype(jnp.bfloat16)
-            span = pl.ds(start, len(fields) * k)
-            rest = send[1, span, :]
-            turned = None
-            for _ in range(3):
-                piece = rest.astype(jnp.bfloat16)
-                rest = rest - piece.astype(jnp.float32)
-                part = jnp.dot(piece, mirror, preferred_element_type=jnp.float32)
-                turned = part if turned is None else turned + part
-            send[1, span, :] = turned
-            if flip:
-                send[1, pl.ds(start, k), :] = -send[1, pl.ds(start, k), :]
+            span = pl.ds(start, count)
+            turned = mirrored(recv[1, span, :])
+            recv[1, span, :] = -turned if flip else turned
 
     each = COLS // (2 * k)
 
@@ -119,9 +122,9 @@
             recv_sem=recv_sem.at[phase, group, land], device_id=target, device_id_type=MESH,
         )
 
-    def row_copies(phase, group, send, recv, span):
-        north = remote(send.at[1, span], recv.at[top_flag, span], phase, group, 1, top_flag, north_id)
-        south = remote(send.at[0, span], recv.at[1, span], phase, group, 0, 1, south_id)
+    def row_copies(phase, group, south_src, north_src, recv, span):
+        north = remote(north_src, recv.at[top_flag, span], phase, group, 1, top_flag, north_id)
+        south = remote(south_src, recv.at[1, span], phase, group, 0, 1, south_id)
         return north, south
 
     def column_copies(phase, group, send, recv):
@@ -136,17 +139,16 @@
         def _():
             pair[1].start()
 
-    def rows_arrive(phase, group, send, recv, span):
-        remote(send.at[1, span], recv.at[1, span], phase, group, 1, 1, north_id).wait_recv()
+    def rows_arrive(phase, group, south_src, north_src, recv, span):
+        remote(north_src, recv.at[1, span], phase, group, 1, 1, north_id).wait_recv()
 
         @pl.when(has_south)
         def _():
-            remote(send.at[0, span], recv.at[0, span], phase, group, 0, 0, south_id).wait_recv()
+            remote(south_src, recv.at[0, span], phase, group, 0, 0, south_id).wait_recv()
 
     per = nt // GROUPS
     groups = range(GROUPS)
-    spans_one = [pl.ds(0, (2 + per) * k)] + [pl.ds((2 + g * per) * k, per * k) for g in groups[1:]]
-    spans_two = [pl.ds(g * per * k, per * k) for g in groups]
+    spans = [pl.ds(g * per * k, per * k) for g in groups]
 
     def place(level, f=0):
         if isinstance(level, int):
@@ -159,25 +161,25 @@
     def put(ref, level, value, f=0):
         ref[place(level, f), :] = value
 
-    for load in loads[:3]:
+    sources = [(v_rows.at[:, 0, :], v_rows.at[:, ROWS - 1, :], ns_recv, pl.ds(0, k))]
+    sources.append((m_rows.at[:, 0, :], m_rows.at[:, ROWS - 1, :], mask_recv, pl.ds(0, k)))
+    for g in groups:
+        span = spans[g]
+        into = pl.ds(k + g * per * k, per * k)
+        sources.append((t_rows.at[span, 0, :], t_rows.at[span, ROWS - 1, :], ns_recv, into))
+    pl.semaphore_wait(barrier, jnp.where(has_south, 4, 3))
+    rows_one = [row_copies(0, i, *source) for i, source in enumerate(sources)]
+    for pair in rows_one[:3]:
+        start_rows(pair)
+    for load in loads[:4]:
         load.wait()
     m[...] = mi[...].astype(jnp.float32)
-    rows_one = []
-    for g in groups:
-        fields = [(t, f * cells) for f in range(g * per, (g + 1) * per)]
-        if g == 0:
-            fields = [(v, 0), (m, 0)] + fields
-        pack_rows(fields, ns_send, spans_one[g].start, g == 0)
-        if g == 0:
-            pl.semaphore_wait(barrier, jnp.where(has_south, 4, 3))
-        rows_one.append(row_copies(0, g, ns_send, ns_recv, spans_one[g]))
-        start_rows(rows_one[g])
-        if g == 0:
-            loads[3].wait()
-            pack_columns([(t, f * cells) for f in range(nt)] + [(u, 0), (m, 0)], ew_send)
-            columns_one = column_copies(0, 0, ew_send, ew_recv)
-            for copy in columns_one:
-                copy.start()
+    pack_columns([(t, f * cells) for f in range(nt)] + [(u, 0), (m, 0)], ew_send)
+    columns_one = column_copies(0, 0, ew_send, ew_recv)
+    for copy in columns_one:
+        copy.start()
+    for pair in rows_one[3:]:
+        start_rows(pair)
     for load in loads[4:]:
         load.wait()
 
@@ -227,7 +229,10 @@
     unpack_columns(ew_recv, y)
 
     def line(which, level, f):
-        return ns_recv[which, pl.ds((2 + f) * k + level, 1), :]
+        return ns_recv[which, pl.ds((1 + f) * k + level, 1), :]
+
+    def wet(which, level):
+        return wide_mask[which, pl.ds(level, 1), :]
 
     def outer_faces(level, carry):
         uu, vv, mm = tile(u, level), tile(v, level), tile(m, level)
@@ -237,12 +242,12 @@
         back = is_open * (lateral_mixing - jnp.minimum(speed, 0.0))
         c_side = jnp.where(lane < COLS // 2, ahead, back)
         c_more = -jnp.where(lane < COLS // 2, back, ahead)
-        speed = 0.5 * (line(0, level, -2) + vv)
-        is_open = jnp.where(row == 0, mm * line(0, level, -1), 0.0)
+        speed = 0.5 * (line(0, level, -1) + vv)
+        is_open = jnp.where(row == 0, mm * wet(0, level), 0.0)
         c_south = is_open * (jnp.maximum(speed, 0.0) + lateral_mixing)
         c_more = c_more - is_open * (lateral_mixing - jnp.minimum(speed, 0.0))
-        speed = 0.5 * (line(1, level, -2) + vv)
-        is_open = jnp.where(row == ROWS - 1, mm * line(1, level, -1), 0.0)
+        speed = 0.5 * (line(1, level, -1) + vv)
+        is_open = jnp.where(row == ROWS - 1, mm * wet(1, level), 0.0)
         c_north = is_open * (lateral_mixing - jnp.minimum(speed, 0.0))
         c_more = c_more - is_open * (jnp.maximum(speed, 0.0) + lateral_mixing)
         for i, c in enumerate((c_side, c_south, c_north, c_more)):
@@ -250,7 +255,7 @@
         put(coef, level, tile(coef, level, 4) + c_more, 4)
         return carry
 
-    rows_two, columns_two = [], []
+    rows_two, columns_two, leaving = [], [], []
     for g in groups:
         mine = range(g * per, (g + 1) * per)
 
@@ -270,13 +275,20 @@
                 put(rhs, level, 0.5 * ((tile(t, level, f) + ss) + stencil(ss, *c)), f)
             return carry
 
-        rows_arrive(0, g, ns_send, ns_recv, spans_one[g])
         if g == 0:
+            rows_arrive(0, 0, *sources[0])
+            rows_arrive(0, 1, *sources[1])
+            wide_mask[...] = mask_recv[...].astype(jnp.float32)
+            fold_rows(ns_recv, 0, k, flip=True)
+            fold_rows(wide_mask, 0, k)
             over_levels(k, outer_faces, 0, k)
+        rows_arrive(0, 2 + g, *sources[2 + g])
+        fold_rows(ns_recv, k + g * per * k, per * k)
         over_levels(k, outer_one, 0, k)
         fields = [(s1, f * cells) for f in mine]
-        pack_rows(fields, ns_send2, g * per * k, False)
-        rows_two.append(row_copies(1, g, ns_send2, ns_recv2, spans_two[g]))
+        pack_rows(fields, ns_send2, g * per * k)
+        leaving.append((ns_send2.at[0, spans[g]], ns_send2.at[1, spans[g]], ns_recv2, spans[g]))
+        rows_two.append(row_copies(1, g, *leaving[g]))
         start_rows(rows_two[g])
         pack_columns(fields, ew_send2.at[g])
         columns_two.append(column_copies(1, g, ew_send2.at[g], ew_recv2.at[g]))
@@ -313,14 +325,16 @@
         for copy in columns_two[g]:
             copy.wait_recv()
         unpack_columns(ew_recv2.at[g], sides)
-        rows_arrive(1, g, ns_send2, ns_recv2, spans_two[g])
+        rows_arrive(1, g, *leaving[g])
+        fold_rows(ns_recv2, g * per * k, per * k)
         over_levels(k, forward, (zero,) * per, k)
         over_levels(k, backward, (zero,) * per, k, backward=True)
 
+    for pair in rows_one:
+        pair[0].wait_send()
     for copy in columns_one:
         copy.wait_send()
     for g in groups:
-        rows_one[g][0].wait_send()
         rows_two[g][0].wait_send()
         for copy in columns_two[g]:
             copy.wait_send()
@@ -343,7 +357,7 @@
     result = pl.pallas_call(
         functools.partial(kernel, nt, k, n_lat, n_lon),
         out_shape=pltpu.VMEM((nt * cells, cols), f32),
-        in_specs=[pl.BlockSpec(memory_space=pltpu.HBM)] * 6,
+        in_specs=[pl.BlockSpec(memory_space=pltpu.HBM)] * 9,
         out_specs=pl.BlockSpec(memory_space=pltpu.VMEM),
         scratch_shapes=[
             vmem(nt * cells, cols),
@@ -360,8 +374,9 @@
             vmem(5 * cells, cols),
             vmem(4 * cells, cols),
             vmem(3 * cells, cols),
-            vmem(2, (nt + 2) * k, cols),
-            vmem(2, (nt + 2) * k, cols),
+            vmem(2, (nt + 1) * k, cols),
+            vmem(2, k, cols, dtype=jnp.int32),
+            vmem(2, k, cols),
             vmem(blocks, rows, cols),
             vmem(2, blocks, rows, cols),
             vmem(2, nt * k, cols),
@@ -369,8 +384,8 @@
             vmem(GROUPS, 1, rows, cols),
             vmem(GROUPS, 2, 1, rows, cols),
             pltpu.SemaphoreType.DMA((6,)),
-            pltpu.SemaphoreType.DMA((2, GROUPS, 4)),
-            pltpu.SemaphoreType.DMA((2, GROUPS, 4)),
+            pltpu.SemaphoreType.DMA((2, GROUPS + 2, 4)),
+            pltpu.SemaphoreType.DMA((2, GROUPS + 2, 4)),
         ],
         compiler_params=pltpu.CompilerParams(
             collective_id=0, has_side_effects=True, vmem_limit_bytes=62 * 1024 * 1024
@@ -382,6 +397,9 @@
         wet_mask.reshape(cells, cols),
         bottom_level,
         vertical_mix.reshape(cells, cols),
+        tracer.reshape(nt * k, rows, cols),
+        north_vel,
+        wet_mask,
     )
     return result.reshape(tracer.shape)
 

time: 14.2 us -> 14.8 us (1.042)
  the two profiles are of different devices: /device:TPU:0 before, /device:TPU:7 now
where the time goes in v5:
time: 14.8 us; the launch traced here: 14.7 us
  Pallas kernels  13.9 us (94%)
  local copies, waits for them, and re-layouts  0.75 us (5%)
    pallas_call x1, Pallas kernels, on_device(): pl.pallas_call(functools.partial(kernel, nt, k, n_lat, n_lon), out_shape=...  13.9 us
    unnamed x1, local copies, waits for them, and re-layouts  0.75 us

profile of v5, /device:TPU:7, one launch (start us, length us, event | category | flops | bytes accessed | tf_op | source)
XLA Modules:
  0.0 14.7 jit_solution(6222812249115989465)
XLA Ops:
  0.0 13.9 %shard_map.64 = f32[768,128]{1,0:T(8,128)S(1)} custom-call(f32[768,128]{1,0:T(8,128)} %bitcast.8, f32[128,128]{1,0:T(8,128)} %bitcast.12, f32[128,128]{1,0:T(8,128)} %bitcast.10, s32[128,128]{1,0:T(8,128)} %bitcast.11, s32[8,128]{1,0:T(8,128)} %b_hbm.1, f32[128,128]{1,0:T(8,128)} %bitcast.13, f32[96,8,128]{2,1,0:T(8,128)} %bitcast.9, f32[16,8,128]{2,1,0:T(8,128)} %v_rows.1, ...), custom_call_target="tpu_custom_call" | custom-call | tf_op jit(solution)/shard_map/pallas_call | solution.py:357
  13.9 0.7 %copy.8 = f32[6,16,8,128]{3,2,1,0:T(8,128)} copy(f32[6,16,8,128]{3,2,1,0:T(8,128)S(1)} %bitcast.7) | data formatting | bytes 786432

commit v6 on v4

--- a/solution.py
+++ b/solution.py
@@ -42,22 +42,27 @@
     top_flag = jnp.where(is_top, 1, 0)
     cells = k * ROWS
 
+    barrier = pltpu.get_barrier_semaphore()
+    for target in ((lat, east), (lat, west), north_id):
+        pl.semaphore_signal(barrier, inc=1, device_id=target, device_id_type=MESH)
+
+    @pl.when(has_south)
+    def _():
+        pl.semaphore_signal(barrier, inc=1, device_id=south_id, device_id_type=MESH)
+
+    per = nt // GROUPS
+    groups = range(GROUPS)
+    spans_one = [pl.ds(0, (2 + per) * k)] + [pl.ds((2 + g * per) * k, per * k) for g in groups[1:]]
+    spans_two = [pl.ds(g * per * k, per * k) for g in groups]
+
+    shares = [pl.ds(g * per * cells, per * cells) for g in groups]
+    pairs = [(m_hbm, mi), (v_hbm, v)] + [(t_hbm.at[share], t.at[share]) for share in shares]
+    pairs += [(u_hbm, u), (b_hbm, b), (mix_hbm, mix)]
     loads = [
-        pltpu.make_async_copy(src, dst, load_sem.at[i])
-        for i, (src, dst) in enumerate(
-            ((t_hbm, t), (v_hbm, v), (m_hbm, mi), (u_hbm, u), (b_hbm, b), (mix_hbm, mix))
-        )
+        pltpu.make_async_copy(src, dst, load_sem.at[i]) for i, (src, dst) in enumerate(pairs)
     ]
     for load in loads:
         load.start()
-
-    barrier = pltpu.get_barrier_semaphore()
-    for target in ((lat, east), (lat, west), north_id):
-        pl.semaphore_signal(barrier, inc=1, device_id=target, device_id_type=MESH)
-
-    @pl.when(has_south)
-    def _():
-        pl.semaphore_signal(barrier, inc=1, device_id=south_id, device_id_type=MESH)
 
     @pl.when(jnp.logical_not(has_south))
     def _():
@@ -68,17 +73,17 @@
     row = lax.broadcasted_iota(jnp.int32, (ROWS, COLS), 0)
     ends = (lane == 0) | (lane == COLS - 1)
 
-    def pack_rows(fields, send, start, flip):
+    def pack_rows(fields, send, start):
         for which, at in ((0, 0), (1, ROWS - 1)):
             for f, (ref, base) in enumerate(fields):
                 send[which, pl.ds(start + f * k, k), :] = ref[pl.ds(base + at, k, stride=ROWS), :]
 
+    def mirror_rows(send, span, flip):
         @pl.when(is_top)
         def _():
             a = lax.broadcasted_iota(jnp.int32, (COLS, COLS), 0)
             c = lax.broadcasted_iota(jnp.int32, (COLS, COLS), 1)
             mirror = jnp.where(a + c == COLS - 1, 1.0, 0.0).astype(jnp.bfloat16)
-            span = pl.ds(start, len(fields) * k)
             rest = send[1, span, :]
             turned = None
             for _ in range(3):
@@ -88,7 +93,7 @@
                 turned = part if turned is None else turned + part
             send[1, span, :] = turned
             if flip:
-                send[1, pl.ds(start, k), :] = -send[1, pl.ds(start, k), :]
+                send[1, pl.ds(0, k), :] = -send[1, pl.ds(0, k), :]
 
     each = COLS // (2 * k)
 
@@ -129,24 +134,20 @@
         to_east = remote(send, recv.at[0], phase, group, 3, 3, (lat, east))
         return to_west, to_east
 
-    def start_rows(pair):
-        pair[0].start()
-
+    def start_rows(pair, send, span, flip):
         @pl.when(has_south)
         def _():
             pair[1].start()
 
+        mirror_rows(send, span, flip)
+        pair[0].start()
+
     def rows_arrive(phase, group, send, recv, span):
         remote(send.at[1, span], recv.at[1, span], phase, group, 1, 1, north_id).wait_recv()
 
         @pl.when(has_south)
         def _():
             remote(send.at[0, span], recv.at[0, span], phase, group, 0, 0, south_id).wait_recv()
-
-    per = nt // GROUPS
-    groups = range(GROUPS)
-    spans_one = [pl.ds(0, (2 + per) * k)] + [pl.ds((2 + g * per) * k, per * k) for g in groups[1:]]
-    spans_two = [pl.ds(g * per * k, per * k) for g in groups]
 
     def place(level, f=0):
         if isinstance(level, int):
@@ -159,7 +160,7 @@
     def put(ref, level, value, f=0):
         ref[place(level, f), :] = value
 
-    for load in loads[:3]:
+    for load in loads[:2]:
         load.wait()
     m[...] = mi[...].astype(jnp.float32)
     rows_one = []
@@ -167,18 +168,19 @@
         fields = [(t, f * cells) for f in range(g * per, (g + 1) * per)]
         if g == 0:
             fields = [(v, 0), (m, 0)] + fields
-        pack_rows(fields, ns_send, spans_one[g].start, g == 0)
+        loads[2 + g].wait()
+        pack_rows(fields, ns_send, spans_one[g].start)
         if g == 0:
             pl.semaphore_wait(barrier, jnp.where(has_south, 4, 3))
         rows_one.append(row_copies(0, g, ns_send, ns_recv, spans_one[g]))
-        start_rows(rows_one[g])
-        if g == 0:
-            loads[3].wait()
+        start_rows(rows_one[g], ns_send, spans_one[g], g == 0)
+        if g == GROUPS - 1:
+            loads[2 + GROUPS].wait()
             pack_columns([(t, f * cells) for f in range(nt)] + [(u, 0), (m, 0)], ew_send)
             columns_one = column_copies(0, 0, ew_send, ew_recv)
             for copy in columns_one:
                 copy.start()
-    for load in loads[4:]:
+    for load in loads[3 + GROUPS :]:
         load.wait()
 
     bottom = b[...]
@@ -275,9 +277,9 @@
             over_levels(k, outer_faces, 0, k)
         over_levels(k, outer_one, 0, k)
         fields = [(s1, f * cells) for f in mine]
-        pack_rows(fields, ns_send2, g * per * k, False)
+        pack_rows(fields, ns_send2, g * per * k)
         rows_two.append(row_copies(1, g, ns_send2, ns_recv2, spans_two[g]))
-        start_rows(rows_two[g])
+        start_rows(rows_two[g], ns_send2, spans_two[g], False)
         pack_columns(fields, ew_send2.at[g])
         columns_two.append(column_copies(1, g, ew_send2.at[g], ew_recv2.at[g]))
         for copy in columns_two[g]:
@@ -368,7 +370,7 @@
             vmem(2, nt * k, cols),
             vmem(GROUPS, 1, rows, cols),
             vmem(GROUPS, 2, 1, rows, cols),
-            pltpu.SemaphoreType.DMA((6,)),
+            pltpu.SemaphoreType.DMA((5 + GROUPS,)),
             pltpu.SemaphoreType.DMA((2, GROUPS, 4)),
             pltpu.SemaphoreType.DMA((2, GROUPS, 4)),
         ],

time: 14.2 us -> 14.3 us (level)
  the two profiles are of different devices: /device:TPU:0 before, /device:TPU:6 now
where the time goes in v6:
time: 14.3 us; the launch traced here: 14.2 us
  Pallas kernels  13.4 us (94%)
  local copies, waits for them, and re-layouts  0.75 us (5%)
    pallas_call x1, Pallas kernels, on_device(): pl.pallas_call(functools.partial(kernel, nt, k, n_lat, n_lon), out_shape=...  13.4 us
    unnamed x1, local copies, waits for them, and re-layouts  0.75 us

profile of v6, /device:TPU:6, one launch (start us, length us, event | category | flops | bytes accessed | tf_op | source)
XLA Modules:
  0.0 14.2 jit_solution(986587941146180430)
XLA Ops:
  0.0 13.4 %shard_map.64 = f32[768,128]{1,0:T(8,128)S(1)} custom-call(f32[768,128]{1,0:T(8,128)} %bitcast.7, f32[128,128]{1,0:T(8,128)} %bitcast.8, f32[128,128]{1,0:T(8,128)} %bitcast.9, s32[128,128]{1,0:T(8,128)} %bitcast.10, s32[8,128]{1,0:T(8,128)} %b_hbm.1, f32[128,128]{1,0:T(8,128)} %bitcast.11), custom_call_target="tpu_custom_call" | custom-call | tf_op jit(solution)/shard_map/pallas_call | solution.py:345
  13.4 0.7 %copy.8 = f32[6,16,8,128]{3,2,1,0:T(8,128)} copy(f32[6,16,8,128]{3,2,1,0:T(8,128)S(1)} %bitcast.6) | data formatting | bytes 786432

commit v7 on v6

--- a/solution.py
+++ b/solution.py
@@ -163,23 +163,22 @@
     for load in loads[:2]:
         load.wait()
     m[...] = mi[...].astype(jnp.float32)
+    for load in loads[2 : 3 + GROUPS]:
+        load.wait()
+    pack_columns([(t, f * cells) for f in range(nt)] + [(u, 0), (m, 0)], ew_send)
+    columns_one = column_copies(0, 0, ew_send, ew_recv)
     rows_one = []
     for g in groups:
         fields = [(t, f * cells) for f in range(g * per, (g + 1) * per)]
         if g == 0:
             fields = [(v, 0), (m, 0)] + fields
-        loads[2 + g].wait()
         pack_rows(fields, ns_send, spans_one[g].start)
         if g == 0:
             pl.semaphore_wait(barrier, jnp.where(has_south, 4, 3))
+            for copy in columns_one:
+                copy.start()
         rows_one.append(row_copies(0, g, ns_send, ns_recv, spans_one[g]))
         start_rows(rows_one[g], ns_send, spans_one[g], g == 0)
-        if g == GROUPS - 1:
-            loads[2 + GROUPS].wait()
-            pack_columns([(t, f * cells) for f in range(nt)] + [(u, 0), (m, 0)], ew_send)
-            columns_one = column_copies(0, 0, ew_send, ew_recv)
-            for copy in columns_one:
-                copy.start()
     for load in loads[3 + GROUPS :]:
         load.wait()
 
@@ -277,13 +276,13 @@
             over_levels(k, outer_faces, 0, k)
         over_levels(k, outer_one, 0, k)
         fields = [(s1, f * cells) for f in mine]
-        pack_rows(fields, ns_send2, g * per * k)
-        rows_two.append(row_copies(1, g, ns_send2, ns_recv2, spans_two[g]))
-        start_rows(rows_two[g], ns_send2, spans_two[g], False)
         pack_columns(fields, ew_send2.at[g])
         columns_two.append(column_copies(1, g, ew_send2.at[g], ew_recv2.at[g]))
         for copy in columns_two[g]:
             copy.start()
+        pack_rows(fields, ns_send2, g * per * k)
+        rows_two.append(row_copies(1, g, ns_send2, ns_recv2, spans_two[g]))
+        start_rows(rows_two[g], ns_send2, spans_two[g], False)
         over_levels(k, inner_two, 0, 8)
 
     for g in groups:

time: 14.3 us -> 14.1 us (0.986)
  the two profiles are of different devices: /device:TPU:6 before, /device:TPU:7 now
where the time goes in v7:
time: 14.1 us; the launch traced here: 13.9 us
  Pallas kernels  13.2 us (94%)
  local copies, waits for them, and re-layouts  0.75 us (5%)
    pallas_call x1, Pallas kernels, on_device(): pl.pallas_call(functools.partial(kernel, nt, k, n_lat, n_lon), out_shape=...  13.2 us
    unnamed x1, local copies, waits for them, and re-layouts  0.75 us

profile of v7, /device:TPU:7, one launch (start us, length us, event | category | flops | bytes accessed | tf_op | source)
XLA Modules:
  0.0 13.9 jit_solution(8989870785250638872)
XLA Ops:
  0.0 13.2 %shard_map.64 = f32[768,128]{1,0:T(8,128)S(1)} custom-call(f32[768,128]{1,0:T(8,128)} %bitcast.7, f32[128,128]{1,0:T(8,128)} %bitcast.8, f32[128,128]{1,0:T(8,128)} %bitcast.9, s32[128,128]{1,0:T(8,128)} %bitcast.10, s32[8,128]{1,0:T(8,128)} %b_hbm.1, f32[128,128]{1,0:T(8,128)} %bitcast.11), custom_call_target="tpu_custom_call" | custom-call | tf_op jit(solution)/shard_map/pallas_call | solution.py:344
  13.2 0.7 %copy.8 = f32[6,16,8,128]{3,2,1,0:T(8,128)} copy(f32[6,16,8,128]{3,2,1,0:T(8,128)S(1)} %bitcast.6) | data formatting | bytes 786432

commit v8 on v7

--- a/solution.py
+++ b/solution.py
@@ -134,13 +134,12 @@
         to_east = remote(send, recv.at[0], phase, group, 3, 3, (lat, east))
         return to_west, to_east
 
-    def start_rows(pair, send, span, flip):
+    def start_rows(pair):
+        pair[0].start()
+
         @pl.when(has_south)
         def _():
             pair[1].start()
-
-        mirror_rows(send, span, flip)
-        pair[0].start()
 
     def rows_arrive(phase, group, send, recv, span):
         remote(send.at[1, span], recv.at[1, span], phase, group, 1, 1, north_id).wait_recv()
@@ -173,12 +172,13 @@
         if g == 0:
             fields = [(v, 0), (m, 0)] + fields
         pack_rows(fields, ns_send, spans_one[g].start)
+        mirror_rows(ns_send, spans_one[g], g == 0)
         if g == 0:
             pl.semaphore_wait(barrier, jnp.where(has_south, 4, 3))
             for copy in columns_one:
                 copy.start()
         rows_one.append(row_copies(0, g, ns_send, ns_recv, spans_one[g]))
-        start_rows(rows_one[g], ns_send, spans_one[g], g == 0)
+        start_rows(rows_one[g])
     for load in loads[3 + GROUPS :]:
         load.wait()
 
@@ -281,8 +281,9 @@
         for copy in columns_two[g]:
             copy.start()
         pack_rows(fields, ns_send2, g * per * k)
+        mirror_rows(ns_send2, spans_two[g], False)
         rows_two.append(row_copies(1, g, ns_send2, ns_recv2, spans_two[g]))
-        start_rows(rows_two[g], ns_send2, spans_two[g], False)
+        start_rows(rows_two[g])
         over_levels(k, inner_two, 0, 8)
 
     for g in groups:

time: 14.1 us -> 14.2 us (level)
  the two profiles are of different devices: /device:TPU:7 before, /device:TPU:0 now
where the time goes in v8:
time: 14.2 us; the launch traced here: 14.1 us
  Pallas kernels  13.3 us (94%)
  local copies, waits for them, and re-layouts  0.75 us (5%)
    pallas_call x1, Pallas kernels, on_device(): pl.pallas_call(functools.partial(kernel, nt, k, n_lat, n_lon), out_shape=...  13.3 us
    unnamed x1, local copies, waits for them, and re-layouts  0.75 us

profile of v8, /device:TPU:0, one launch (start us, length us, event | category | flops | bytes accessed | tf_op | source)
XLA Modules:
  0.0 14.1 jit_solution(3768941604391680294)
XLA Ops:
  0.0 13.3 %shard_map.64 = f32[768,128]{1,0:T(8,128)S(1)} custom-call(f32[768,128]{1,0:T(8,128)} %bitcast.7, f32[128,128]{1,0:T(8,128)} %bitcast.8, f32[128,128]{1,0:T(8,128)} %bitcast.9, s32[128,128]{1,0:T(8,128)} %bitcast.10, s32[8,128]{1,0:T(8,128)} %b_hbm.1, f32[128,128]{1,0:T(8,128)} %bitcast.11), custom_call_target="tpu_custom_call" | custom-call | tf_op jit(solution)/shard_map/pallas_call | solution.py:345
  13.3 0.7 %copy.8 = f32[6,16,8,128]{3,2,1,0:T(8,128)} copy(f32[6,16,8,128]{3,2,1,0:T(8,128)S(1)} %bitcast.6) | data formatting | bytes 786432
